TPU v7x, 128 devices: a whole 4x4x4 slice. The times are simulated.
128 devices in a mesh: group: 2 (over y_lo), lat: 8 (over y_hi, z), lon: 8 (over x, core).
Axes of the slice: x: 4, y: 4 (y_hi: 2, y_lo: 2; y = y_hi * 2 + y_lo), z: 4, core: 2. Of those that a mesh axis runs over, the one named last changes fastest.
Arguments:
- atmos: bfloat16 [256, 720, 1024], P('group', 'lat', 'lon'), may hold values from -6 to 6
- cotangent: bfloat16 [256, 720, 1024], P('group', 'lat', 'lon'), may hold values from -6 to 6
- ocean: bfloat16 [76, 720, 1024], P(None, 'lat', 'lon'), may hold values from -6 to 6
- sea_mask: int32 [720, 1024], P('lat', 'lon'), may hold values 0 or 1
- spectral_weight: float32 [256, 384], P(('group', 'lat', 'lon')), may hold values from -5 to 5
- coupling: float32 [256], P('group'), may hold values from -5 to 5
- flux_weight: bfloat16 [4, 256], P(None, 'group'), may hold values from -0.375 to 0.375
- conv_weight: bfloat16 [3, 3, 80, 256], P(None, None, None, 'group'), may hold values from -0.21875 to 0.21875
- head_weight: bfloat16 [256, 76], P('group'), may hold values from -0.375 to 0.375
Outputs:
- atmos_next: bfloat16 [256, 720, 1024], P('group', 'lat', 'lon')
- grad_atmos: bfloat16 [256, 720, 1024], P('group', 'lat', 'lon')
- grad_spectral: float32 [256, 384], P(('group', 'lat', 'lon'))
- ocean_next: bfloat16 [76, 720, 1024], P(None, 'lat', 'lon')
All inputs are finite; a program needn't handle non-finite values. No bound on the sum of `sea_mask` on one device may be relied on, other than what follows from the above.
Results may differ from a plain program's by a relative error of at most 0.012.
Values may be sent and summed in bfloat16 or wider, within the bound.
No kernel may reach another device: no remote copies, remote signals or barrier semaphores. Data moves between devices by JAX's collectives and lax.ppermute only.
A program may use at most 192 MiB of HBM per device.

v0:
```python
import math

import jax
import jax.numpy as jnp
from jax import lax
from jax.sharding import PartitionSpec as P

NLAT = 720
NLON = 1024
KMODES = 384
LDEG = 384


def padded_2(cells, sides, width):
    for axis, dim in sides:
        count = lax.axis_size(axis)
        head = lax.slice_in_dim(cells, 0, width, axis=dim)
        tail = lax.slice_in_dim(cells, cells.shape[dim] - width, cells.shape[dim], axis=dim)
        cells = jnp.concatenate(
            [
                lax.ppermute(tail, axis, [(i, (i + 1) % count) for i in range(count)]),
                cells,
                lax.ppermute(head, axis, [((i + 1) % count, i) for i in range(count)]),
            ],
            axis=dim,
        )
    return cells


def make_tables(nlat, nlon, kmodes, ldeg):
    column = jnp.arange(nlon, dtype=jnp.int32)[:, None]
    wavenum = jnp.arange(kmodes, dtype=jnp.int32)[None, :]
    phase_cos = (column * wavenum % nlon).astype(jnp.float32) * (2.0 * math.pi / nlon)
    phase_sin = (column * (wavenum + 1) % nlon).astype(jnp.float32) * (2.0 * math.pi / nlon)
    lon_table = (
        jnp.concatenate([jnp.cos(phase_cos), jnp.sin(phase_sin)], axis=1) * math.sqrt(2.0 / nlon)
    ).astype(jnp.bfloat16)
    latrow = jnp.arange(nlat, dtype=jnp.int32)[:, None]
    degree = jnp.arange(ldeg, dtype=jnp.int32)[None, :]
    phase_lat = (degree * (2 * latrow + 1) % (4 * nlat)).astype(jnp.float32) * (
        math.pi / (2 * nlat)
    )
    lat_table = (jnp.cos(phase_lat) * math.sqrt(2.0 / nlat)).astype(jnp.bfloat16)
    return (lon_table, lat_table)


def lon_forward(fields, lon_table):
    return jnp.einsum(
        "fcan,nk->fcak", fields, lon_table, preferred_element_type=jnp.float32
    ).astype(jnp.bfloat16)


def lon_inverse(lat_back, lon_table):
    return jnp.einsum(
        "fcak,nk->fcan", lat_back, lon_table, preferred_element_type=jnp.float32
    ).astype(jnp.bfloat16)


def spectral_middle(lon_coef, lat_table, weights):
    spectra = jnp.einsum("fcak,al->fclk", lon_coef, lat_table, preferred_element_type=jnp.float32)
    filtered = (spectra * weights[None, :, :, None]).astype(jnp.bfloat16)
    lat_back = jnp.einsum(
        "fclk,al->fcak", filtered, lat_table, preferred_element_type=jnp.float32
    ).astype(jnp.bfloat16)
    return (lat_back, spectra)


def swap_blocks(fields, first, second):
    shape = fields.shape
    split = fields.reshape((shape[0], first, second, shape[1] // (first * second)) + shape[2:])
    return split.transpose(0, 2, 1, 3, 4, 5).reshape(shape)


def convolve(padded, conv_weight, row_count, columns):
    summed = jnp.zeros((conv_weight.shape[3], row_count, columns), jnp.float32)
    for row_shift in range(3):
        for col_shift in range(3):
            window = padded[:, row_shift : row_shift + row_count, col_shift : col_shift + columns]
            summed = summed + jnp.einsum(
                "irq,ih->hrq",
                window,
                conv_weight[row_shift, col_shift],
                preferred_element_type=jnp.float32,
            )
    return jax.nn.gelu(summed).astype(jnp.bfloat16)


def local(
    atmos,
    cotangent,
    ocean,
    sea_mask,
    spectral_weight,
    coupling,
    flux_weight,
    conv_weight,
    head_weight,
):
    lat_count = lax.axis_size("lat")
    lon_count = lax.axis_size("lon")
    rows = atmos.shape[1]
    columns = atmos.shape[2]
    sea_cells = sea_mask.astype(jnp.float32)
    atmos_input = (
        atmos.astype(jnp.float32)
        + sea_cells[None] * ocean[0].astype(jnp.float32)[None] * coupling[:, None, None]
    ).astype(jnp.bfloat16)
    fields = jnp.stack([atmos_input, cotangent])
    lon_table, lat_table = make_tables(NLAT, NLON, KMODES, LDEG)
    whole = lax.all_to_all(
        lax.all_to_all(fields, "lat", split_axis=1, concat_axis=2, tiled=True),
        "lon",
        split_axis=1,
        concat_axis=3,
        tiled=True,
    )
    lat_back, spectra = spectral_middle(lon_forward(whole, lon_table), lat_table, spectral_weight)
    returned = lax.all_to_all(
        lax.all_to_all(
            lon_inverse(lat_back, lon_table), "lat", split_axis=2, concat_axis=1, tiled=True
        ),
        "lon",
        split_axis=3,
        concat_axis=1,
        tiled=True,
    )
    back = swap_blocks(returned, lon_count, lat_count)
    grad_spectral = jnp.sum(spectra[0] * spectra[1], axis=-1) / KMODES
    atmos_next = (atmos_input.astype(jnp.float32) + back[0].astype(jnp.float32)).astype(
        jnp.bfloat16
    )
    grad_atmos = (cotangent.astype(jnp.float32) + back[1].astype(jnp.float32)).astype(jnp.bfloat16)
    flux_part = jnp.einsum(
        "fc,crq->frq", flux_weight, atmos_next, preferred_element_type=jnp.float32
    )
    flux = lax.psum(flux_part.astype(jnp.bfloat16), "group")
    ocean_input = jnp.concatenate([ocean, flux], axis=0)
    padded = padded_2(ocean_input, (("lat", 1), ("lon", 2)), 1)
    lat_index = lax.axis_index("lat")
    row_index = jnp.arange(rows + 2, dtype=jnp.int32)
    at_pole = (row_index == 0) & (lat_index == 0) | (row_index == rows + 1) & (
        lat_index == lat_count - 1
    )
    padded = jnp.where(at_pole[None, :, None], jnp.zeros_like(padded), padded)
    hidden = convolve(padded, conv_weight, rows, columns)
    delta_part = jnp.einsum("hrq,ho->orq", hidden, head_weight, preferred_element_type=jnp.float32)
    delta = lax.psum(delta_part.astype(jnp.bfloat16), "group").astype(jnp.float32)
    ocean_next = (ocean.astype(jnp.float32) + sea_cells[None] * delta).astype(jnp.bfloat16)
    return (atmos_next, grad_atmos, grad_spectral, ocean_next)


def solution(mesh):
    in_specs = (
        P("group", "lat", "lon"),
        P("group", "lat", "lon"),
        P(None, "lat", "lon"),
        P("lat", "lon"),
        P(("group", "lat", "lon"), None),
        P("group"),
        P(None, "group"),
        P(None, None, None, "group"),
        P("group", None),
    )
    out_specs = (
        P("group", "lat", "lon"),
        P("group", "lat", "lon"),
        P(("group", "lat", "lon"), None),
        P(None, "lat", "lon"),
    )
    return jax.shard_map(local, mesh=mesh, in_specs=in_specs, out_specs=out_specs, check_vma=False)
```

profile of v0, /device:TPU:1, one launch (start us, length us, event | category | flops | bytes accessed | tf_op | source)
XLA Modules:
  0.0 709.2 jit_solution(10448927505836321836)
XLA Ops:
  9.1 3.0 fusion.76
  12.6 43.9 %copy.52 = bf16[2,128,90,128]{3,0,2,1:T(2,128)(2,1)S(1)} copy(bf16[2,128,90,128]{3,1,2,0:T(8,128)(2,1)S(1)} %pad_maximum_fusion) | data formatting | bytes 11796480 | tf_op jit(solution)/shard_map/stack | solution.py:108
  56.6 75.9 %all_to_all.69 = bf16[2,128,90,128]{3,0,2,1:T(2,128)(2,1)S(1)} all-to-all(bf16[2,128,90,128]{3,0,2,1:T(2,128)(2,1)S(1)} %copy.52), channel_id=1, replica_groups=mesh['group'=2,'lat'=8,'lon'=8] {'lat'}, dimensions={1} | all-to-all | bytes 11796480 | tf_op jit(solution)/shard_map/all_to_all | solution.py:111
  132.5 1.5 copy.53
  135.1 4.1 copy.55
  139.1 7.1 %all-to-all-start.1 = ((bf16[2,16,720,128]{3,2,0,1:T(8,128)(2,1)}), bf16[2,16,720,128]{3,2,0,1:T(8,128)(2,1)}, u32[]{:S(2)}, u32[]{:S(2)}) async-start(bf16[2,16,720,128]{3,2,0,1:T(8,128)(2,1)} %copy.55), calls=%async_computation.1 | async-start | bytes 11796480 | tf_op jit(solution)/shard_map/all_to_all | solution.py:110
  146.7 11.4 %fusion.53 = (f32[1024,384]{1,0:T(8,128)S(1)}, f32[1024,384]{1,0:T(8,128)S(1)}) fusion(s32[384]{0:T(512)S(1)} %iota_add_fusion), kind=kLoop, calls=%fused_computation.63 | loop fusion | flops 11010048 | bytes 3147264 | tf_op jit(solution)/shard_map/cos | solution.py:36
  158.0 55.4 %all-to-all-done.1 = bf16[2,16,720,128]{3,2,0,1:T(8,128)(2,1)} async-done(((bf16[2,16,720,128]{3,2,0,1:T(8,128)(2,1)}), bf16[2,16,720,128]{3,2,0,1:T(8,128)(2,1)}, u32[]{:S(2)}, u32[]{:S(2)}) %all-to-all-start.1) | async-done | bytes 5898272 | tf_op jit(solution)/shard_map/all_to_all | solution.py:110
  213.4 20.2 %copy.81 = bf16[2,8,2,720,128]{4,1,3,2,0:T(8,128)(2,1)} copy(bf16[2,8,2,720,128]{4,3,0,2,1:T(8,128)(2,1)} %bitcast.9) | data formatting | bytes 11796480 | tf_op jit(solution)/shard_map/all_to_all | solution.py:110
  233.7 9.9 %all_to_all.57 = bf16[2,2,720,1024]{3,2,1,0:T(8,128)(2,1)} reshape(bf16[2,2,720,8,128]{4,3,2,1,0:T(8,128)(2,1)} %bitcast.121) | data formatting | bytes 11796480 | tf_op jit(solution)/shard_map/all_to_all | solution.py:110
  243.6 18.4 %fusion.25 = f32[2,2,384,768]{3,2,1,0:T(8,128)} fusion(bf16[2,2,720,1024]{3,2,1,0:T(8,128)(2,1)} %all_to_all.57, s32[720]{0:T(1024)S(1)} %multiply_add_fusion, f32[1024,384]{1,0:T(8,128)S(1)} %get-tuple-element.11, f32[1024,384]{1,0:T(8,128)S(1)} %get-tuple-element.10), kind=kOutput, calls=%fused_computation.39 | convolution fusion | flops 6236153856 | bytes 13765440 | tf_op jit(solution)/shard_map/fcak,al->fclk/dot_general | solution.py:60
  262.0 15.5 %fusion.13 = bf16[2,2,720,1024]{3,2,1,0:T(8,128)(2,1)} fusion(f32[2,2,384,768]{3,2,1,0:T(8,128)} %fusion.25, f32[2,384]{1,0:T(2,128)S(1)} %copy-done.10, s32[720]{0:T(1024)S(1)} %multiply_add_fusion, f32[1024,384]{1,0:T(8,128)S(1)} %get-tuple-element.11, f32[1024,384]{1,0:T(8,128)S(1)} %get-tuple-element.10), kind=kOutput, calls=%fused_computation.22 | convolution fusion | flops 6241462272 | bytes 13768512 | tf_op jit(solution)/shard_map/fcak,nk->fcan/dot_general | solution.py:54
  277.5 28.9 %copy.57 = bf16[2,2,720,1024]{3,1,0,2:T(2,128)(2,1)S(1)} copy(bf16[2,2,720,1024]{3,2,1,0:T(8,128)(2,1)} %fusion.13) | data formatting | bytes 11796480 | tf_op jit(solution)/shard_map/convert_element_type | solution.py:56
  306.5 70.2 %all_to_all.70 = bf16[2,2,720,1024]{3,1,0,2:T(2,128)(2,1)S(1)} all-to-all(bf16[2,2,720,1024]{3,1,0,2:T(2,128)(2,1)S(1)} %copy.57), channel_id=1, replica_groups=mesh['group'=2,'lat'=8,'lon'=8] {'lat'}, dimensions={2} | all-to-all | bytes 11796480 | tf_op jit(solution)/shard_map/all_to_all | solution.py:119
  376.7 4.9 copy.59
  381.6 14.5 %copy.60 = bf16[2,16,90,1024]{2,1,0,3:T(8,128)(2,1)} copy(bf16[2,16,90,1024]{3,0,2,1:T(2,128)(2,1)} %bitcast.117) | data formatting | bytes 11796480 | tf_op jit(solution)/shard_map/all_to_all | solution.py:119
  396.1 103.5 %all_to_all.71 = bf16[2,16,90,1024]{2,1,0,3:T(8,128)(2,1)} all-to-all(bf16[2,16,90,1024]{2,1,0,3:T(8,128)(2,1)} %copy.60), channel_id=1, replica_groups=mesh['group'=2,'lat'=8,'lon'=8] {'lon'}, dimensions={3} | all-to-all | bytes 11796480 | tf_op jit(solution)/shard_map/all_to_all | solution.py:118
  499.6 9.9 %copy.62 = bf16[2,8,16,90,128]{4,1,3,2,0:T(8,128)(2,1)} copy(bf16[2,8,16,90,128]{3,2,0,4,1:T(8,128)(2,1)} %bitcast.115) | data formatting | bytes 11796480 | tf_op jit(solution)/shard_map/all_to_all | solution.py:118
  509.5 6.0 slice_convert_fusion
  515.5 5.7 copy.63
  521.3 5.0 add_convert_fusion.1
  526.3 1.6 copy-done.4
  527.9 1.1 fusion.67
  529.1 24.2 %all-reduce.3.cloned.1.call-done = bf16[4,90,128]{2,0,1:T(4,128)(2,1)} async-done(((bf16[4,90,128]{2,0,1:T(4,128)(2,1)}), bf16[4,90,128]{2,0,1:T(4,128)(2,1)}) %all-reduce.3.cloned.1.call-update) | async-done | bytes 92176 | tf_op jit(solution)/shard_map/psum | solution.py:136
  554.0 4.9 collective-permute-start.1
  559.8 5.3 collective-permute-done
  566.2 2.5 fusion.137
  568.7 2.3 copy.66
  571.0 2.5 collective-permute-start.3
  573.5 2.3 copy.65
  575.7 1.1 collective-permute-start.2
  576.9 2.0 copy.68
  578.9 2.0 copy.67
  580.9 6.8 maximum_select_fusion
  587.8 4.2 fusion.30
  592.0 3.5 fusion.32
  595.4 4.2 fusion.34
  599.6 4.1 fusion.36
  603.7 3.5 fusion.38
  607.2 4.0 fusion.40
  611.2 3.6 fusion.44
  614.8 4.0 fusion.42
  618.8 19.6 %convert_bitcast_fusion = bf16[76,90,128]{2,0,1:T(8,128)(2,1)} fusion(f32[90,128,128]{2,1,0:T(8,128)} %fusion.30, f32[90,128,128]{2,1,0:T(8,128)} %fusion.32, f32[90,128,128]{2,1,0:T(8,128)} %fusion.34, f32[90,128,128]{2,1,0:T(8,128)} %fusion.36, f32[90,128,128]{2,1,0:T(8,128)} %fusion.38, f32[90,128,128]{2,1,0:T(8,128)} %fusion.40, ...), kind=kOutput, calls=%fused_computation.58 | convolution fusion | flops 486005760 | bytes 50821120 | tf_op jit(solution)/shard_map/hrq,ho->orq/dot_general | solution.py:146
  638.5 2.7 fusion.22
  641.8 6.5 copy.64
  648.3 4.7 add_convert_fusion
  652.9 45.6 %all-reduce.5.cloned.1.call-done = bf16[76,90,128]{2,0,1:T(8,128)(2,1)} async-done(((bf16[76,90,128]{2,0,1:T(8,128)(2,1)}), bf16[76,90,128]{2,0,1:T(8,128)(2,1)}) %all-reduce.5.cloned.1.call-update) | async-done | bytes 1751056 | tf_op jit(solution)/shard_map/psum | solution.py:147
  698.5 3.4 add_convert_fusion.3
  (40 shorter events, 7.3 us)
Async XLA Ops:
  7.2 611.7 %copy-start = (bf16[128,76]{0,1:T(8,128)(2,1)S(1)}, bf16[128,76]{0,1:T(8,128)(2,1)}, u32[]{:S(2)}) copy-start(bf16[128,76]{0,1:T(8,128)(2,1)} %param.17) | copy-start | bytes 58372
  7.2 4.9 copy-start.3
  139.1 74.3 %all-to-all-start.1 = ((bf16[2,16,720,128]{3,2,0,1:T(8,128)(2,1)}), bf16[2,16,720,128]{3,2,0,1:T(8,128)(2,1)}, u32[]{:S(2)}, u32[]{:S(2)}) async-start(bf16[2,16,720,128]{3,2,0,1:T(8,128)(2,1)} %copy.55), calls=%async_computation.1 | async-start | bytes 11796480 | tf_op jit(solution)/shard_map/all_to_all | solution.py:110
  146.3 407.0 %all-reduce.3.cloned.1.call-start = ((), (), s32[]{:S(2)}) async-start(), calls=%async_computation.4 | async-start | bytes 184320 | tf_op jit(solution)/shard_map/psum | solution.py:136
  243.6 18.4 %copy-start.10 = (f32[2,384]{1,0:T(2,128)S(1)}, f32[2,384]{1,0:T(2,128)}, u32[]{:S(2)}) copy-start(f32[2,384]{1,0:T(2,128)} %param.13) | copy-start | bytes 9220
  515.5 5.7 copy-start.8
  521.3 6.7 copy-start.9
  526.3 1.6 copy-start.4
  527.9 25.4 %copy-start.2 = (bf16[76,90,128]{2,0,1:T(8,128)(2,1)S(1)}, bf16[76,90,128]{2,0,1:T(8,128)(2,1)}, u32[]{:S(2)}) copy-start(bf16[76,90,128]{2,0,1:T(8,128)(2,1)} %param.11) | copy-start | bytes 5253124
  529.1 169.5 %all-reduce.5.cloned.1.call-start = ((), (), s32[]{:S(2)}) async-start(), calls=%async_computation.5 | async-start | bytes 3686400 | tf_op jit(solution)/shard_map/psum | solution.py:147
  554.0 5.8 collective-permute-start.1
  558.8 6.2 collective-permute-start
  568.7 12.2 %copy-start.5 = (bf16[4,90,128]{2,0,1:T(4,128)(2,1)S(1)}, bf16[4,90,128]{2,0,1:T(4,128)(2,1)}, u32[]{:S(2)}) copy-start(bf16[4,90,128]{2,0,1:T(4,128)(2,1)} %all-reduce.3.cloned.1.call-done) | copy-start | bytes 276484
  571.0 5.9 collective-permute-start.3
  575.7 3.2 collective-permute-start.2
  580.9 6.9 copy-start.7
  587.8 27.0 %copy-start.1 = (bf16[80,92,130]{2,0,1:T(8,128)(2,1)}, bf16[80,92,130]{2,0,1:T(8,128)(2,1)S(1)}, u32[]{:S(2)}) copy-start(bf16[80,92,130]{2,0,1:T(8,128)(2,1)S(1)} %maximum_select_fusion) | copy-start | bytes 5740804
  618.8 19.7 %copy-start.6 = (s32[90,128]{1,0:T(8,128)S(1)}, s32[90,128]{1,0:T(8,128)}, u32[]{:S(2)}) copy-start(s32[90,128]{1,0:T(8,128)} %param.12) | copy-start | bytes 138244
Sparse Core Ops, SparseCore 0:
  529.2 24.0 all-reduce.2
  638.6 59.8 all-reduce.4
where the time goes:
time: 715 us; the launch traced here: 709 us
  blocking collectives  250 us (35%)
  local copies, waits for them, and re-layouts  165 us (23%)
  waiting for transfers between devices  131 us (18%)
  matrix products  85.7 us (12%)
  other arithmetic  46.6 us (7%)
  starting transfers between devices  16 us (2%)
  between operations  14.7 us (2%)
    all_to_all x1, blocking collectives, local(): lax.all_to_all(lax.all_to_all(lon_inverse(lat_back, lon_table), 'lat', sp...  103 us
    all_to_all x1, blocking collectives, local(): lax.all_to_all(fields, 'lat', split_axis=1, concat_axis=2, tiled=True)  75.9 us
    all_to_all x1, blocking collectives, local(): lax.all_to_all(lon_inverse(lat_back, lon_table), 'lat', split_axis=2, con...  70.2 us
    all_to_all x1, waiting for transfers between devices, local(): lax.all_to_all(lax.all_to_all(fields, 'lat', split_axis=1, concat_axis=2,...  55.4 us
    psum x1, waiting for transfers between devices, local(): lax.psum(delta_part.astype(jnp.bfloat16), 'group').astype(jnp.float32)  45.6 us
    another operation x1, local copies, waits for them, and re-layouts, local(): fields = jnp.stack([atmos_input, cotangent])  43.9 us
    dot_general x8, matrix products, convolve(): jnp.einsum('irq,ih->hrq', window, conv_weight[row_shift, col_shift], pref...  31 us
    all_to_all x2, local copies, waits for them, and re-layouts, local(): lax.all_to_all(lax.all_to_all(fields, 'lat', split_axis=1, concat_axis=2,...  30.2 us
  transfers between devices with their start and end apart: 7, of which 5 were waited for; matrix products, arithmetic and copies ran while one was open for 4% of the time, Pallas kernels for 0%

commit v1 on v0

v1 whole, which is shorter than its diff:
```python
import math

import jax
import jax.numpy as jnp
from jax import lax
from jax.experimental import pallas as pl
from jax.experimental.pallas import tpu as pltpu
from jax.sharding import PartitionSpec as P

NLAT = 720
NLON = 1024
KMODES = 384
LDEG = 384
ROWS = 90
COLS = 128
CH = 128
OWNERS = 64
SENT = 360
BACK = 368
F32 = jnp.float32
BF16 = jnp.bfloat16
VMEM_LIMIT = 58 * 1024 * 1024


def make_tables(nlat, nlon, kmodes, ldeg):
    column = jnp.arange(nlon, dtype=jnp.int32)[:, None]
    wavenum = jnp.arange(kmodes, dtype=jnp.int32)[None, :]
    phase_cos = (column * wavenum % nlon).astype(jnp.float32) * (2.0 * math.pi / nlon)
    phase_sin = (column * (wavenum + 1) % nlon).astype(jnp.float32) * (2.0 * math.pi / nlon)
    lon_table = (
        jnp.concatenate([jnp.cos(phase_cos), jnp.sin(phase_sin)], axis=1) * math.sqrt(2.0 / nlon)
    ).astype(jnp.bfloat16)
    latrow = jnp.arange(nlat, dtype=jnp.int32)[:, None]
    degree = jnp.arange(ldeg, dtype=jnp.int32)[None, :]
    phase_lat = (degree * (2 * latrow + 1) % (4 * nlat)).astype(jnp.float32) * (
        math.pi / (2 * nlat)
    )
    lat_table = (jnp.cos(phase_lat) * math.sqrt(2.0 / nlat)).astype(jnp.bfloat16)
    return (lon_table, lat_table)


def arrange_lat(lat_table):
    blocks = lat_table.reshape(4, 2, ROWS, LDEG)
    main = blocks[:, :, :80].reshape(4, 160, LDEG)
    middle = blocks[:, :, 80:88].reshape(4, 16, LDEG)
    last = blocks[:, :, None, 88:90]
    made = []
    for m in range(4):
        own = (jnp.arange(4) == m)[None, None, :, None, None]
        tail = jnp.where(own, last, jnp.zeros_like(last)).reshape(4, 16, LDEG)
        made.append(jnp.concatenate([main, middle, tail], axis=1).reshape(768, LDEG))
    return jnp.stack(made)


def pack_kernel(atmos, cotangent, ocean, mask, coupling, out, held_a, held_c, last):
    step = pl.program_id(0)
    gain = jnp.broadcast_to(coupling[...], (CH, COLS)).T
    forcing = mask[...].astype(F32) * ocean[:, 0, :].astype(F32)
    for r in range(16):
        held_a[r * CH : (r + 1) * CH, :] = atmos[r].astype(F32) + forcing[r : r + 1, :] * gain
        held_c[r * CH : (r + 1) * CH, :] = cotangent[r].astype(F32)

    @pl.when(step < 5)
    def _():
        for ch in range(CH):
            for f, held in enumerate((held_a, held_c)):
                at = 32 * f + 16 * (ch % 2)
                out[ch // 2, at : at + 16, :] = held[pl.ds(ch, 16, stride=CH), :].astype(BF16)

    @pl.when(step == 5)
    def _():
        for d in range(OWNERS):
            for f, held in enumerate((held_a, held_c)):
                pair = [held[pl.ds(2 * d + c, 8, stride=CH), :] for c in range(2)]
                out[d, 16 * f : 16 * f + 16, :] = jnp.concatenate(pair, axis=0).astype(BF16)
                for t in range(2):
                    both = held[(8 + t) * CH + 2 * d : (8 + t) * CH + 2 * d + 2, :]
                    for c in range(2):
                        row = 4 * f + 2 * c + t
                        last[row : row + 1, :] = both[c : c + 1]
            out[d, 32:40, :] = last[...].astype(BF16)


def pack(atmos, cotangent, ocean, sea_mask, coupling):
    return pl.pallas_call(
        pack_kernel,
        grid=(6,),
        in_specs=[
            pl.BlockSpec((16, CH, COLS), lambda i: (i, 0, 0)),
            pl.BlockSpec((16, CH, COLS), lambda i: (i, 0, 0)),
            pl.BlockSpec((16, 16, COLS), lambda i: (i, 0, 0)),
            pl.BlockSpec((16, COLS), lambda i: (i, 0)),
            pl.BlockSpec((1, CH), lambda i: (0, 0)),
        ],
        out_specs=pl.BlockSpec((OWNERS, 64, COLS), lambda i: (0, i, 0)),
        out_shape=jax.ShapeDtypeStruct((OWNERS, SENT, COLS), BF16),
        scratch_shapes=[
            pltpu.VMEM((16 * CH, COLS), F32),
            pltpu.VMEM((16 * CH, COLS), F32),
            pltpu.VMEM((8, COLS), F32),
        ],
        compiler_params=pltpu.CompilerParams(vmem_limit_bytes=VMEM_LIMIT),
        name="pack",
    )(atmos, cotangent, ocean, sea_mask, coupling[None, :])


def spectral_kernel(
    got, lon, lon_back, lat, lat_back, weight, out, grad, coef, kept, back, edge_in, edge, halo
):
    step = pl.program_id(0)

    @pl.when(step == 0)
    def _():
        edge_in[...] = jnp.zeros_like(edge_in)
        edge[...] = jnp.zeros_like(edge)

    @pl.when(step < 4)
    def _():
        for n in range(3):
            cols = slice(256 * n, 256 * n + 256)
            found = []
            for a in range(2):
                rows = jnp.concatenate([got[8 * a + o] for o in range(8)], axis=1)
                found.append(jnp.dot(rows, lon[:, cols], preferred_element_type=F32))
            for m in range(4):
                for a in range(2):
                    for i in range(5):
                        coef[m, step, 80 * a + 16 * i : 80 * a + 16 * i + 16, cols] = found[a][
                            64 * i + 16 * m : 64 * i + 16 * m + 16
                        ].astype(BF16)
                coef[m, step, 160:176, cols] = jnp.concatenate(
                    [found[a][320 + 8 * m : 328 + 8 * m] for a in range(2)], axis=0
                ).astype(BF16)
                coef[m, step, 176:192, cols] = jnp.concatenate(
                    [found[a][352:360] for a in range(2)], axis=0
                ).astype(BF16)
        for a in range(2):
            block = 2 * step + a
            for o in range(8):
                lanes = slice(128 * o, 128 * o + 128)
                low = got[8 * a + o, 352:360, :].astype(F32)
                for c in range(2):
                    high = got[8 * a + o, 16 * c : 16 * c + 16, :].astype(F32)
                    edge_in[block + 2, c : c + 1, lanes] = low[2 * c + 1 : 2 * c + 2]
                    edge_in[block, 2 + c : 3 + c, lanes] = high[0:1]

    @pl.when(step == 4)
    def _():
        for c in range(2):
            scale = jnp.concatenate([weight[c], weight[c]], axis=1)
            total = jnp.zeros((LDEG, 128), F32)
            for n in range(3):
                cols = slice(256 * n, 256 * n + 256)
                spectra = []
                for f in range(2):
                    m = 2 * f + c
                    held = coef[m, :, :, cols].reshape(768, 256)
                    found = jnp.dot(lat[m], held, preferred_element_type=F32)
                    kept[m, :, cols] = (found * scale).astype(BF16)
                    spectra.append(found)
                product = spectra[0] * spectra[1]
                total = total + product[:, :128] + product[:, 128:]
            grad[c : c + 1, :] = jnp.sum(total.T, axis=0, keepdims=True) / KMODES
        for n in range(3):
            cols = slice(256 * n, 256 * n + 256)
            tails = [jnp.zeros((16, 256), F32) for _ in range(4)]
            for m in range(4):
                found = jnp.dot(lat_back[m], kept[m, :, cols], preferred_element_type=F32)
                for p in range(4):
                    base = 192 * p
                    back[p, 160 * m : 160 * m + 160, cols] = found[base : base + 160].astype(BF16)
                    back[p, 640 + 16 * m : 656 + 16 * m, cols] = found[
                        base + 160 : base + 176
                    ].astype(BF16)
                    tail = found[base + 176 : base + 192]
                    tails[p] = tails[p] + tail
                    if m < 2:
                        for a in range(2):
                            block = 2 * p + a
                            row = 8 * a + 2 * m + 1
                            edge[block + 2, m : m + 1, cols] = tail[row : row + 1]
                            edge[block, 2 + m : 3 + m, cols] = found[
                                base + 80 * a : base + 80 * a + 1
                            ]
            for p in range(4):
                back[p, 704:720, cols] = tails[p].astype(BF16)
        outside = edge[1:9].reshape(64, 768).astype(BF16)
        halo[...] = (
            jnp.dot(outside, lon_back[...], preferred_element_type=F32)
            + edge_in[1:9].reshape(64, NLON)
        ).reshape(8, 8, NLON)

    @pl.when(step >= 4)
    def _():
        p = step - 4
        rows = back[p]
        for n in range(4):
            cols = slice(256 * n, 256 * n + 256)
            found = jnp.dot(rows, lon_back[:, cols], preferred_element_type=F32)
            for half in range(2):
                o = 2 * n + half
                lanes = slice(128 * half, 128 * half + 128)
                for a in range(2):
                    d = 8 * a + o
                    for i in range(5):
                        for m in range(4):
                            at = 160 * m + 80 * a + 16 * i
                            to = 64 * i + 16 * m
                            out[d, to : to + 16, :] = (
                                found[at : at + 16, lanes] + got[d, to : to + 16, :].astype(F32)
                            ).astype(BF16)
                    for f in range(2):
                        at = 640 + 32 * f + 8 * a
                        to = 320 + 16 * f
                        pair = jnp.concatenate(
                            [found[at : at + 8, lanes], found[at + 16 : at + 24, lanes]], axis=0
                        )
                        out[d, to : to + 16, :] = (
                            pair + got[d, to : to + 16, :].astype(F32)
                        ).astype(BF16)
                    at = 704 + 8 * a
                    low = found[at : at + 8, lanes] + got[d, 352:360, :].astype(F32)
                    beyond = halo[2 * p + a, :, 128 * o : 128 * o + 128]
                    out[d, 352:368, :] = jnp.concatenate([low, beyond], axis=0).astype(BF16)


def spectral(got, lon, lon_back, lat, lat_back, weight):
    once = pl.Buffered(1)
    return pl.pallas_call(
        spectral_kernel,
        grid=(8,),
        in_specs=[
            pl.BlockSpec((16, SENT, COLS), lambda g: (g % 4, 0, 0)),
            pl.BlockSpec((NLON, 768), lambda g: (0, 0), pipeline_mode=once),
            pl.BlockSpec((768, NLON), lambda g: (0, 0), pipeline_mode=once),
            pl.BlockSpec((4, LDEG, 768), lambda g: (0, 0, 0), pipeline_mode=once),
            pl.BlockSpec((4, 768, LDEG), lambda g: (0, 0, 0), pipeline_mode=once),
            pl.BlockSpec((2, LDEG, 128), lambda g: (0, 0, 0), pipeline_mode=once),
        ],
        out_specs=[
            pl.BlockSpec((16, BACK, COLS), lambda g: (jnp.maximum(g - 4, 0), 0, 0)),
            pl.BlockSpec((2, LDEG), lambda g: (0, 0)),
        ],
        out_shape=[
            jax.ShapeDtypeStruct((OWNERS, BACK, COLS), BF16),
            jax.ShapeDtypeStruct((2, LDEG), F32),
        ],
        scratch_shapes=[
            pltpu.VMEM((4, 4, 192, 768), BF16),
            pltpu.VMEM((4, LDEG, 768), BF16),
            pltpu.VMEM((4, 720, 768), BF16),
            pltpu.VMEM((10, 8, NLON), F32),
            pltpu.VMEM((10, 8, 768), F32),
            pltpu.VMEM((8, 8, NLON), F32),
        ],
        compiler_params=pltpu.CompilerParams(vmem_limit_bytes=VMEM_LIMIT),
        cost_estimate=pl.CostEstimate(
            flops=12_500_000_000, bytes_accessed=20_000_000, transcendentals=0
        ),
        name="spectral",
    )(got, lon, lon_back, lat, lat_back, weight)


def spread(main, middle, low, held, field):
    step = pl.program_id(0)

    @pl.when(step < 5)
    def _():
        for ch in range(CH):
            at = 16 * (ch % 2)
            held[pl.ds(ch, 16, stride=CH), :] = main[ch // 2, at : at + 16, :].astype(F32)

    @pl.when(step == 5)
    def _():
        for d in range(OWNERS):
            near = middle[d].astype(F32)
            last = low[d].astype(F32)
            for c in range(2):
                held[pl.ds(2 * d + c, 8, stride=CH), :] = near[8 * c : 8 * c + 8]
                for t in range(2):
                    row = 4 * field + 2 * c + t
                    at = (8 + t) * CH + 2 * d + c
                    held[at : at + 1, :] = last[row : row + 1]


def unpack_flux_kernel(main, middle, low, weight, out, flux, held, outside):
    step = pl.program_id(0)
    spread(main, middle, low, held, 0)
    out[...] = held[...].reshape(16, CH, COLS).astype(BF16)

    def put(row, cells):
        found = jnp.dot(weight[...], cells, preferred_element_type=F32)
        flux[row] = found[0:4].astype(BF16)

    @pl.when(step < 5)
    def _():
        for r in range(16):
            put(1 + 16 * step + r, out[r])

    @pl.when(step == 5)
    def _():
        for r in range(10):
            put(81 + r, out[r])
        for d in range(OWNERS):
            beyond = low[d].astype(F32)
            for side in range(2):
                outside[side, 2 * d : 2 * d + 2, :] = beyond[8 + 2 * side : 10 + 2 * side]
        put(0, outside[0].astype(BF16))
        put(91, outside[1].astype(BF16))


def unpack_kernel(main, middle, low, out, held):
    spread(main, middle, low, held, 1)
    out[...] = held[...].reshape(16, CH, COLS).astype(BF16)


def unpack_specs(field):
    return [
        pl.BlockSpec((OWNERS, 32, COLS), lambda i: (0, 2 * jnp.minimum(i, 4) + field, 0)),
        pl.BlockSpec((OWNERS, 16, COLS), lambda i: (0, 20 + field, 0)),
        pl.BlockSpec((OWNERS, 16, COLS), lambda i: (0, 22, 0)),
    ]


def unpack_flux(sent_back, weight):
    return pl.pallas_call(
        unpack_flux_kernel,
        grid=(6,),
        in_specs=unpack_specs(0) + [pl.BlockSpec((16, CH), lambda i: (0, 0))],
        out_specs=[
            pl.BlockSpec((16, CH, COLS), lambda i: (i, 0, 0)),
            pl.BlockSpec((ROWS + 2, 4, COLS), lambda i: (0, 0, 0)),
        ],
        out_shape=[
            jax.ShapeDtypeStruct((ROWS, CH, COLS), BF16),
            jax.ShapeDtypeStruct((ROWS + 2, 4, COLS), BF16),
        ],
        scratch_shapes=[pltpu.VMEM((16 * CH, COLS), F32), pltpu.VMEM((2, CH, COLS), F32)],
        compiler_params=pltpu.CompilerParams(vmem_limit_bytes=VMEM_LIMIT),
        name="unpack_flux",
    )(sent_back, sent_back, sent_back, weight)


def unpack(sent_back):
    return pl.pallas_call(
        unpack_kernel,
        grid=(6,),
        in_specs=unpack_specs(1),
        out_specs=pl.BlockSpec((16, CH, COLS), lambda i: (i, 0, 0)),
        out_shape=jax.ShapeDtypeStruct((ROWS, CH, COLS), BF16),
        scratch_shapes=[pltpu.VMEM((16 * CH, COLS), F32)],
        compiler_params=pltpu.CompilerParams(vmem_limit_bytes=VMEM_LIMIT),
        cost_estimate=pl.CostEstimate(flops=0, bytes_accessed=6_000_000, transcendentals=0),
        name="unpack",
    )(sent_back, sent_back, sent_back)


def ocean_kernel(
    taps, more, own, other, left, left_other, right, right_other, conv, head, ocean, mask, out, fluxes
):
    step = pl.program_id(0)

    @pl.when(step == 0)
    def _():
        def whole(one, two):
            total = one[...].astype(F32) + two[...].astype(F32)
            return total.astype(BF16).astype(F32)

        lane = lax.broadcasted_iota(jnp.int32, (ROWS + 2, 4, COLS), 2)
        middle = whole(own, other)
        west = whole(left, left_other)
        east = whole(right, right_other)
        fluxes[:, 0:4, :] = jnp.where(
            lane == 0, pltpu.roll(west, 1, 2), pltpu.roll(middle, 1, 2)
        )
        fluxes[:, 4:8, :] = middle
        fluxes[:, 8:12, :] = jnp.where(
            lane == COLS - 1, pltpu.roll(east, COLS - 1, 2), pltpu.roll(middle, COLS - 1, 2)
        )
        fluxes[:, 12:16, :] = jnp.zeros((ROWS + 2, 4, COLS), F32)

    def cells(row):
        known = taps[row, 0:240, :] if row < 10 else more[row - 10, 0:240, :]
        return jnp.concatenate([known, fluxes[10 * step + row].astype(BF16)], axis=0)

    for pair in range(5):
        rows = [cells(2 * pair + k) for k in range(4)]
        around = jnp.concatenate(
            [jnp.concatenate(rows[0:3], axis=0), jnp.concatenate(rows[1:4], axis=0)], axis=1
        )
        summed = jnp.dot(conv[...], around, preferred_element_type=F32)
        hidden = jax.nn.gelu(summed).astype(BF16)
        delta = jnp.dot(head[...], hidden, preferred_element_type=F32)
        for k in range(2):
            row = 2 * pair + k
            sea = mask[pl.ds(10 * step + row, 1), :].astype(F32)
            out[row] = (
                ocean[row].astype(F32) + sea * delta[0:76, COLS * k : COLS * k + COLS]
            ).astype(BF16)


def ocean_step(taps, fluxes, conv, head, ocean, sea_mask):
    flux_spec = pl.BlockSpec((ROWS + 2, 4, COLS), lambda g: (0, 0, 0))
    return pl.pallas_call(
        ocean_kernel,
        grid=(9,),
        in_specs=[
            pl.BlockSpec((10, 256, COLS), lambda g: (g, 0, 0)),
            pl.BlockSpec((2, 256, COLS), lambda g: (5 * g + 5, 0, 0)),
        ]
        + [flux_spec] * 6
        + [
            pl.BlockSpec((256, 768), lambda g: (0, 0)),
            pl.BlockSpec((80, 256), lambda g: (0, 0)),
            pl.BlockSpec((10, 76, COLS), lambda g: (g, 0, 0)),
            pl.BlockSpec((ROWS, COLS), lambda g: (0, 0)),
        ],
        out_specs=pl.BlockSpec((10, 76, COLS), lambda g: (g, 0, 0)),
        out_shape=jax.ShapeDtypeStruct((ROWS, 76, COLS), BF16),
        scratch_shapes=[pltpu.VMEM((ROWS + 2, 16, COLS), F32)],
        compiler_params=pltpu.CompilerParams(vmem_limit_bytes=VMEM_LIMIT),
        name="ocean",
    )(taps, taps, *fluxes, conv, head, ocean, sea_mask)


def after(value, *others):
    return lax.optimization_barrier((value,) + others)[0]


def local(
    atmos,
    cotangent,
    ocean,
    sea_mask,
    spectral_weight,
    coupling,
    flux_weight,
    conv_weight,
    head_weight,
):
    atmos = atmos.transpose(1, 0, 2)
    cotangent = cotangent.transpose(1, 0, 2)
    ocean = ocean.transpose(1, 0, 2)
    ring = range(8)
    east = [(k, (k + 1) % 8) for k in ring]
    west = [((k + 1) % 8, k) for k in ring]
    swap = [(0, 1), (1, 0)]

    sent = pack(atmos, cotangent, ocean, sea_mask, coupling)
    got = lax.all_to_all(sent, ("lat", "lon"), split_axis=0, concat_axis=0, tiled=True)

    lon_table, lat_table = make_tables(NLAT, NLON, KMODES, LDEG)
    lat_back = arrange_lat(lat_table)
    lat = lat_back.transpose(0, 2, 1)
    scale = jnp.broadcast_to(spectral_weight[:, :, None], (2, LDEG, 128))
    hidden_weights = jnp.concatenate(
        [conv_weight.reshape(720, 128), head_weight.T], axis=0
    )
    hidden_weights = after(hidden_weights, sent)
    weights = jnp.concatenate(
        [hidden_weights, lax.ppermute(hidden_weights, "group", swap)], axis=1
    )
    below = after(ocean[ROWS - 1 :], sent)
    above = after(ocean[:1], sent)
    top = lax.ppermute(below, "lat", [(k, k + 1) for k in range(7)])
    bottom = lax.ppermute(above, "lat", [(k + 1, k) for k in range(7)])
    conv = weights[:720].reshape(3, 3, 80, 256)
    conv = jnp.concatenate(
        [
            conv[:, :, :76].reshape(3, 3, 76, 256),
            jnp.zeros((3, 3, 4, 256), BF16),
        ],
        axis=2,
    ).reshape(3, 240, 256)
    conv_flux = weights[:720].reshape(3, 3, 80, 256)[:, :, 76:].reshape(3, 12, 256)
    conv = jnp.concatenate([conv, conv_flux, jnp.zeros((3, 4, 256), BF16)], axis=1)
    conv = conv.reshape(768, 256).T
    head = jnp.concatenate([weights[720:], jnp.zeros((4, 256), BF16)], axis=0)
    flux_rows = jnp.concatenate([flux_weight, jnp.zeros((12, CH), BF16)], axis=0)

    sent_back, grad_spectral = spectral(got, lon_table, lon_table.T, lat, lat_back, scale)
    returned = lax.all_to_all(sent_back, ("lat", "lon"), split_axis=0, concat_axis=0, tiled=True)

    tall = after(jnp.concatenate([top, ocean, bottom], axis=0), sent_back)
    first = lax.ppermute(tall[:, :, COLS - 1], "lon", east)[:, :, None]
    final = lax.ppermute(tall[:, :, 0], "lon", west)[:, :, None]
    wide = jnp.concatenate([first, tall, final], axis=2)
    taps = jnp.stack([wide[:, :, b : b + COLS] for b in range(3)], axis=1)
    taps = jnp.pad(taps, ((0, 8), (0, 0), (0, 4), (0, 0))).reshape(100, 240, COLS)
    taps = jnp.pad(taps, ((0, 0), (0, 16), (0, 0)))

    atmos_next, flux = unpack_flux(returned, flux_rows)
    across = [(8 * g + k, 8 * (1 - g) + (k + 1) % 8) for g in range(2) for k in ring]
    counter = [(8 * g + k, 8 * (1 - g) + (k - 1) % 8) for g in range(2) for k in ring]
    fluxes = [
        flux,
        lax.ppermute(flux, "group", swap),
        lax.ppermute(flux, "lon", east),
        lax.ppermute(flux, ("group", "lon"), across),
        lax.ppermute(flux, "lon", west),
        lax.ppermute(flux, ("group", "lon"), counter),
    ]
    grad_atmos = unpack(after(returned, flux))
    ocean_next = ocean_step(taps, fluxes, conv, head, ocean, sea_mask)
    return (
        atmos_next.transpose(1, 0, 2),
        grad_atmos.transpose(1, 0, 2),
        grad_spectral,
        ocean_next.transpose(1, 0, 2),
    )


def solution(mesh):
    in_specs = (
        P("group", "lat", "lon"),
        P("group", "lat", "lon"),
        P(None, "lat", "lon"),
        P("lat", "lon"),
        P(("group", "lat", "lon"), None),
        P("group"),
        P(None, "group"),
        P(None, None, None, "group"),
        P("group", None),
    )
    out_specs = (
        P("group", "lat", "lon"),
        P("group", "lat", "lon"),
        P(("group", "lat", "lon"), None),
        P(None, "lat", "lon"),
    )
    return jax.shard_map(local, mesh=mesh, in_specs=in_specs, out_specs=out_specs, check_vma=False)
```

time: 715 us -> 297 us (0.42)
  the two profiles are of different devices: /device:TPU:1 before, /device:TPU:66 now
where the time goes in v1:
time: 297 us; the launch traced here: 292 us
  waiting for transfers between devices  127 us (43%)
  Pallas kernels  69.3 us (23%)
  starting transfers between devices  33 us (11%)
  other arithmetic  33 us (11%)
  local copies, waits for them, and re-layouts  28.4 us (10%)
    all_to_all x1, waiting for transfers between devices, local(): lax.all_to_all(sent, ('lat', 'lon'), split_axis=0, concat_axis=0, tiled=T...  50.2 us
    ppermute x1, waiting for transfers between devices, local(): bottom = lax.ppermute(above, 'lat', [(k + 1, k) for k in range(7)])  42 us
    ppermute x1, waiting for transfers between devices, local(): lax.ppermute(hidden_weights, 'group', swap)  22.8 us
    pallas_call x1, Pallas kernels, spectral(): pl.pallas_call(spectral_kernel, grid=(8,), in_specs=[pl.BlockSpec((16, SE...  21.4 us
    pallas_call x1, Pallas kernels, ocean_step(): pl.pallas_call(ocean_kernel, grid=(9,), in_specs=[pl.BlockSpec((10, 256,...  20.6 us
    cos x1, other arithmetic, make_tables(): jnp.cos(phase_cos)  11.7 us
    ppermute x1, waiting for transfers between devices, local(): top = lax.ppermute(below, 'lat', [(k, k + 1) for k in range(7)])  11 us
    all_to_all x1, starting transfers between devices, local(): lax.all_to_all(sent, ('lat', 'lon'), split_axis=0, concat_axis=0, tiled=T...  10.8 us
  transfers between devices with their start and end apart: 12, of which 5 were waited for; matrix products, arithmetic and copies ran while one was open for 20% of the time, Pallas kernels for 3%

profile of v1, /device:TPU:66, one launch (start us, length us, event | category | flops | bytes accessed | tf_op | source)
XLA Modules:
  0.0 292.0 jit_solution(10503918856216275332)
XLA Ops:
  0.6 10.6 %pack.1 = bf16[64,360,128]{2,1,0:T(8,128)(2,1)} custom-call(bf16[90,128,128]{2,1,0:T(8,128)(2,1)} %bitcast.41, bf16[90,128,128]{2,1,0:T(8,128)(2,1)} %bitcast.42, bf16[90,76,128]{2,1,0:T(8,128)(2,1)} %bitcast.36, s32[90,128]{1,0:T(8,128)} %mask.3, f32[1,128]{1,0:T(1,128)} %bitcast.59), custom_call_target="tpu_custom_call" | custom-call | tf_op jit(solution)/shard_map/pack/pallas_call | solution.py:85
  11.2 10.8 %all-to-all-start = ((bf16[64,360,128]{2,1,0:T(8,128)(2,1)}), bf16[64,360,128]{2,1,0:T(8,128)(2,1)}, u32[]{:S(2)}, u32[]{:S(2)}) async-start(bf16[64,360,128]{2,1,0:T(8,128)(2,1)} %pack.1), calls=%async_computation | async-start | bytes 11796480 | tf_op jit(solution)/shard_map/all_to_all | solution.py:450
  22.0 5.2 %fusion.21 = bf16[4,2,90,384]{3,2,1,0:T(8,128)(2,1)S(1)} fusion(s32[4,2,90]{2,1,0:T(2,128)S(1)} %multiply_add_fusion), kind=kLoop, calls=%fused_computation.34 | loop fusion | flops 3041280 | bytes 555840 | tf_op jit(solution)/shard_map/convert_element_type | solution.py:38
  27.6 0.1 broadcast_in_dim.125
  28.1 0.1 broadcast_select_fusion.4
  28.2 0.3 pad_maximum_fusion.5
  28.5 1.7 pad_maximum_fusion.1
  30.2 3.1 %copy.27.lat = bf16[4,384,768]{2,1,0:T(8,128)(2,1)} copy(bf16[4,384,768]{1,2,0:T(8,128)(2,1)S(1)} %get-tuple-element.23) | data formatting | bytes 4718592 | tf_op jit(solution)/shard_map/transpose | solution.py:454
  33.3 11.7 %fusion.6 = (f32[1024,384]{0,1:T(8,128)S(1)}, f32[1024,384]{0,1:T(8,128)S(1)}) fusion(s32[384]{0:T(512)S(1)} %iota_add_fusion), kind=kLoop, calls=%fused_computation.19 | loop fusion | flops 11010048 | bytes 3147264 | tf_op jit(solution)/shard_map/cos | solution.py:31
  45.0 1.6 fusion
  46.6 2.6 copy.26.lon
  49.2 1.6 fusion.28.lon_back
  50.8 50.2 %all-to-all-done.got = bf16[64,360,128]{2,1,0:T(8,128)(2,1)} async-done(((bf16[64,360,128]{2,1,0:T(8,128)(2,1)}), bf16[64,360,128]{2,1,0:T(8,128)(2,1)}, u32[]{:S(2)}, u32[]{:S(2)}) %all-to-all-start) | async-done | bytes 5898272 | tf_op jit(solution)/shard_map/all_to_all | solution.py:450
  101.0 0.9 broadcast_in_dim.133.weight
  101.9 21.4 %spectral.1 = (bf16[64,368,128]{2,1,0:T(8,128)(2,1)}, f32[2,384]{1,0:T(2,128)}) custom-call(bf16[64,360,128]{2,1,0:T(8,128)(2,1)} %all-to-all-done.got, bf16[1024,768]{1,0:T(8,128)(2,1)} %copy.26.lon, bf16[768,1024]{1,0:T(8,128)(2,1)} %fusion.28.lon_back, bf16[4,384,768]{2,1,0:T(8,128)(2,1)} %copy.27.lat, bf16[4,768,384]{2,1,0:T(8,128)(2,1)} %get-tuple-element.22.lat_back, ...), custom_call_target="tpu_custom_call" | custom-call | flops 12499999744 | bytes 20000000 | tf_op jit(solution)/shard_map/spectral/pallas_call | solution.py:229
  123.4 10.1 %all-to-all-start.1 = ((bf16[64,368,128]{2,1,0:T(8,128)(2,1)}), bf16[64,368,128]{2,1,0:T(8,128)(2,1)}, u32[]{:S(2)}, u32[]{:S(2)}) async-start(bf16[64,368,128]{2,1,0:T(8,128)(2,1)} %get-tuple-element.13), calls=%async_computation.1 | async-start | bytes 12058624 | tf_op jit(solution)/shard_map/all_to_all | solution.py:482
  133.4 0.8 fusion.27
  134.2 3.1 %collective-permute-start = (bf16[1,76,128]{2,1,0:T(8,128)(2,1)S(1)}, bf16[1,76,128]{2,1,0:T(8,128)(2,1)S(1)}, u32[]{:S(2)}, u32[]{:S(2)}) collective-permute-start(bf16[1,76,128]{2,1,0:T(8,128)(2,1)S(1)} %get-tuple-element.18), channel_id=1, source_target_pairs={{0,8},{8,16},{16,24},{24,32},{32,40},{40,48},{48,56},{1,9},{9,17},... | collective-permute-start | bytes 58376 | tf_op jit(solution)/shard_map/ppermute | solution.py:465
  137.3 2.7 collective-permute-start.1
  140.3 0.6 concatenate.48.weight
  141.0 11.0 %collective-permute-done = bf16[1,76,128]{2,1,0:T(8,128)(2,1)S(1)} collective-permute-done((bf16[1,76,128]{2,1,0:T(8,128)(2,1)S(1)}, bf16[1,76,128]{2,1,0:T(8,128)(2,1)S(1)}, u32[]{:S(2)}, u32[]{:S(2)}) %collective-permute-start) | collective-permute-done | bytes 19488 | tf_op jit(solution)/shard_map/ppermute | solution.py:465
  152.0 42.0 %collective-permute-done.1 = bf16[1,76,128]{2,1,0:T(8,128)(2,1)S(1)} collective-permute-done((bf16[1,76,128]{2,1,0:T(8,128)(2,1)S(1)}, bf16[1,76,128]{2,1,0:T(8,128)(2,1)S(1)}, u32[]{:S(2)}, u32[]{:S(2)}) %collective-permute-start.1) | collective-permute-done | bytes 19488 | tf_op jit(solution)/shard_map/ppermute | solution.py:466
  194.0 1.8 pad_maximum_fusion.4
  195.8 22.8 %collective-permute-done.9 = bf16[796,128]{1,0:T(8,128)(2,1)S(1)} collective-permute-done((bf16[796,128]{1,0:T(8,128)(2,1)S(1)}, bf16[796,128]{1,0:T(8,128)(2,1)S(1)}, u32[]{:S(2)}, u32[]{:S(2)}) %collective-permute-start.9) | collective-permute-done | bytes 203808 | tf_op jit(solution)/shard_map/ppermute | solution.py:461
  218.7 0.1 broadcast_select_fusion
  218.8 2.5 fusion.26
  221.3 2.4 copy.28
  223.8 2.3 copy.30
  226.0 0.5 collective-permute-start.2
  226.5 0.1 maximum_maximum_fusion
  226.7 0.6 concatenate.56.head
  227.3 0.9 copy.33
  228.2 1.0 collective-permute-done.2
  229.3 2.0 copy.29
  231.3 2.0 copy.31
  233.3 6.0 %fusion.2 = (bf16[92,1,76,128]{3,2,0,1:T(8,128)(2,1)}, bf16[92,1,76,128]{3,2,0,1:T(8,128)(2,1)}) fusion(bf16[92,76,128]{2,1,0:T(8,128)(2,1)S(1)} %pad_maximum_fusion.4, bf16[92,76,1]{2,1,0:T(8,128)(2,1)} %copy.29, bf16[92,76,1]{2,1,0:T(8,128)(2,1)} %copy.31), kind=kLoop, calls=%fused_computation.13 | loop fusion | flops 7159808 | bytes 5397824 | tf_op jit(solution)/shard_map/stack | solution.py:488
  239.2 8.9 %unpack_flux.1 = (bf16[90,128,128]{2,1,0:T(8,128)(2,1)}, bf16[92,4,128]{2,1,0:T(4,128)(2,1)}) custom-call(bf16[64,368,128]{2,1,0:T(8,128)(2,1)} %all-to-all-done.1.main.middle.low, bf16[64,368,128]{2,1,0:T(8,128)(2,1)} %all-to-all-done.1.main.middle.low, bf16[64,368,128]{2,1,0:T(8,128)(2,1)} %all-to-all-done.1.main.middle.low, ...), custom_call_target="tpu_custom_call" | custom-call | tf_op jit(solution)/shard_map/unpack_flux/pallas_call | solution.py:326
  248.1 2.2 collective-permute-start.8
  250.3 0.5 collective-permute-start.6
  250.7 0.9 collective-permute-start.5
  251.7 2.3 collective-permute-start.4
  253.9 2.9 pad_maximum_fusion
  256.8 1.0 copy.34
  257.8 1.0 pad.11.clone
  258.8 3.7 %pad.12.taps.more = bf16[100,256,128]{2,1,0:T(8,128)(2,1)} pad(bf16[100,240,128]{2,1,0:T(8,128)(2,1)S(1)} %bitcast.35, bf16[]{:T(256)} %constant.60.clone.1), padding=0_0x0_16x0_0 | pad | bytes 12697602 | tf_op jit(solution)/shard_map/jit(_pad)/pad | solution.py:490
  262.6 7.8 %unpack.1 = bf16[90,128,128]{2,1,0:T(8,128)(2,1)} custom-call(bf16[64,368,128]{2,1,0:T(8,128)(2,1)} %all-to-all-done.1.main.middle.low, bf16[64,368,128]{2,1,0:T(8,128)(2,1)} %all-to-all-done.1.main.middle.low, bf16[64,368,128]{2,1,0:T(8,128)(2,1)} %all-to-all-done.1.main.middle.low), custom_call_target="tpu_custom_call" | custom-call | bytes 6000000 | tf_op jit(solution)/shard_map/unpack/pallas_call | solution.py:345
  270.4 0.5 copy-done.2
  271.1 20.6 %ocean.1 = bf16[90,76,128]{2,1,0:T(8,128)(2,1)} custom-call(bf16[100,256,128]{2,1,0:T(8,128)(2,1)} %pad.12.taps.more, bf16[100,256,128]{2,1,0:T(8,128)(2,1)} %pad.12.taps.more, bf16[92,4,128]{2,1,0:T(4,128)(2,1)} %get-tuple-element.15.own, bf16[92,4,128]{2,1,0:T(4,128)(2,1)} %copy-done.6, bf16[92,4,128]{2,1,0:T(4,128)(2,1)} %copy-done.5, ...), custom_call_target="tpu_custom_call" | custom-call | tf_op jit(solution)/shard_map/ocean/pallas_call | solution.py:404
  (60 shorter events, 1.4 us)
Async XLA Ops:
  11.2 89.7 %all-to-all-start = ((bf16[64,360,128]{2,1,0:T(8,128)(2,1)}), bf16[64,360,128]{2,1,0:T(8,128)(2,1)}, u32[]{:S(2)}, u32[]{:S(2)}) async-start(bf16[64,360,128]{2,1,0:T(8,128)(2,1)} %pack.1), calls=%async_computation | async-start | bytes 11796480 | tf_op jit(solution)/shard_map/all_to_all | solution.py:450
  49.2 51.7 %copy-start.8 = (f32[2,384]{1,0:T(2,128)S(1)}, f32[2,384]{1,0:T(2,128)}, u32[]{:S(2)}) copy-start(f32[2,384]{1,0:T(2,128)} %param.13) | copy-start | bytes 9220
  123.3 16.7 %copy-start.1 = (bf16[3,3,80,128]{3,2,1,0:T(8,128)(2,1)S(1)}, bf16[3,3,80,128]{3,2,1,0:T(8,128)(2,1)}, u32[]{:S(2)}) copy-start(bf16[3,3,80,128]{3,2,1,0:T(8,128)(2,1)} %param.16) | copy-start | bytes 552964
  123.3 16.7 %copy-start.7 = (bf16[128,76]{0,1:T(8,128)(2,1)S(1)}, bf16[128,76]{0,1:T(8,128)(2,1)}, u32[]{:S(2)}) copy-start(bf16[128,76]{0,1:T(8,128)(2,1)} %param.17) | copy-start | bytes 58372
  123.3 16.9 %copy-start.10 = (pred[80]{0:T(512)(128)(4,1)S(1)}, pred[80]{0:T(512)(128)(4,1)}, u32[]{:S(2)}) copy-start(pred[80]{0:T(512)(128)(4,1)} %constant.62.clone.1) | copy-start | bytes 244
  123.3 17.0 %copy-start.9 = (bf16[4,128]{1,0:T(4,128)(2,1)S(1)}, bf16[4,128]{1,0:T(4,128)(2,1)}, u32[]{:S(2)}) copy-start(bf16[4,128]{1,0:T(4,128)(2,1)} %param.15) | copy-start | bytes 3076
  123.4 115.9 %all-to-all-start.1 = ((bf16[64,368,128]{2,1,0:T(8,128)(2,1)}), bf16[64,368,128]{2,1,0:T(8,128)(2,1)}, u32[]{:S(2)}, u32[]{:S(2)}) async-start(bf16[64,368,128]{2,1,0:T(8,128)(2,1)} %get-tuple-element.13), calls=%async_computation.1 | async-start | bytes 12058624 | tf_op jit(solution)/shard_map/all_to_all | solution.py:482
  134.2 17.8 %collective-permute-start = (bf16[1,76,128]{2,1,0:T(8,128)(2,1)S(1)}, bf16[1,76,128]{2,1,0:T(8,128)(2,1)S(1)}, u32[]{:S(2)}, u32[]{:S(2)}) collective-permute-start(bf16[1,76,128]{2,1,0:T(8,128)(2,1)S(1)} %get-tuple-element.18), channel_id=1, source_target_pairs={{0,8},{8,16},{16,24},{24,32},{32,40},{40,48},{48,56},{1,9},{9,17},... | collective-permute-start | bytes 58376 | tf_op jit(solution)/shard_map/ppermute | solution.py:465
  137.3 56.7 %collective-permute-start.1 = (bf16[1,76,128]{2,1,0:T(8,128)(2,1)S(1)}, bf16[1,76,128]{2,1,0:T(8,128)(2,1)S(1)}, u32[]{:S(2)}, u32[]{:S(2)}) collective-permute-start(bf16[1,76,128]{2,1,0:T(8,128)(2,1)S(1)} %get-tuple-element.19), channel_id=1, source_target_pairs={{8,0},{16,8},{24,16},{32,24},{40,32},{48,40},{56,48},{9,1},{17,9},... | collective-permute-start | bytes 58376 | tf_op jit(solution)/shard_map/ppermute | solution.py:466
  140.1 78.5 %collective-permute-start.9 = (bf16[796,128]{1,0:T(8,128)(2,1)S(1)}, bf16[796,128]{1,0:T(8,128)(2,1)S(1)}, u32[]{:S(2)}, u32[]{:S(2)}) collective-permute-start(bf16[796,128]{1,0:T(8,128)(2,1)S(1)} %pad_maximum_fusion.10), channel_id=1, source_target_pairs={{0,64},{64,0},{1,65},{65,1},{2,66},{66,2},{3,67},{67,3},{4,68},{68... | collective-permute-start | bytes 611336 | tf_op jit(solution)/shard_map/ppermute | solution.py:461
  226.0 5.3 %collective-permute-start.3 = (bf16[92,76]{0,1:T(8,128)(2,1)S(1)}, bf16[92,76]{0,1:T(8,128)(2,1)S(1)}, u32[]{:S(2)}, u32[]{:S(2)}) collective-permute-start(bf16[92,76]{0,1:T(8,128)(2,1)S(1)} %bitcast.55), channel_id=1, source_target_pairs={{1,0},{2,1},{3,2},{4,3},{5,4},{6,5},{7,6},{0,7},{9,8},{10,9},{11,1... | collective-permute-start | bytes 41960 | tf_op jit(solution)/shard_map/ppermute | solution.py:486
  226.0 3.2 %collective-permute-start.2 = (bf16[92,76]{0,1:T(8,128)(2,1)S(1)}, bf16[92,76]{0,1:T(8,128)(2,1)S(1)}, u32[]{:S(2)}, u32[]{:S(2)}) collective-permute-start(bf16[92,76]{0,1:T(8,128)(2,1)S(1)} %bitcast.57), channel_id=1, source_target_pairs={{0,1},{1,2},{2,3},{3,4},{4,5},{5,6},{6,7},{7,0},{8,9},{9,10},{10,1... | collective-permute-start | bytes 41960 | tf_op jit(solution)/shard_map/ppermute | solution.py:485
  239.2 14.7 %copy-start = (bf16[92,1,76,128]{3,2,0,1:T(8,128)(2,1)S(1)}, bf16[92,1,76,128]{3,2,0,1:T(8,128)(2,1)}, u32[]{:S(2)}) copy-start(bf16[92,1,76,128]{3,2,0,1:T(8,128)(2,1)} %get-tuple-element.24) | copy-start | bytes 5369860
  248.1 22.2 %collective-permute-start.8 = (bf16[92,4,128]{2,1,0:T(4,128)(2,1)}, bf16[92,4,128]{2,1,0:T(4,128)(2,1)S(1)}, u32[]{:S(2)}, u32[]{:S(2)}) collective-permute-start(bf16[92,4,128]{2,1,0:T(4,128)(2,1)} %get-tuple-element.15.own), channel_id=1, source_target_pairs={{0,71},{1,64},{2,65},{3,66},{4,67},{5,68},{6,69},{7,70},{64,7},{65... | collective-permute-start | bytes 282632 | tf_op jit(solution)/shard_map/ppermute | solution.py:501
  250.3 20.1 %collective-permute-start.7 = (bf16[92,4,128]{2,1,0:T(4,128)(2,1)}, bf16[92,4,128]{2,1,0:T(4,128)(2,1)S(1)}, u32[]{:S(2)}, u32[]{:S(2)}) collective-permute-start(bf16[92,4,128]{2,1,0:T(4,128)(2,1)} %get-tuple-element.15.own), channel_id=1, source_target_pairs={{1,0},{2,1},{3,2},{4,3},{5,4},{6,5},{7,6},{0,7},{9,8},{10,9},{11,1... | collective-permute-start | bytes 282632 | tf_op jit(solution)/shard_map/ppermute | solution.py:500
  250.3 20.1 %collective-permute-start.6 = (bf16[92,4,128]{2,1,0:T(4,128)(2,1)}, bf16[92,4,128]{2,1,0:T(4,128)(2,1)S(1)}, u32[]{:S(2)}, u32[]{:S(2)}) collective-permute-start(bf16[92,4,128]{2,1,0:T(4,128)(2,1)} %get-tuple-element.15.own), channel_id=1, source_target_pairs={{0,65},{1,66},{2,67},{3,68},{4,69},{5,70},{6,71},{7,64},{64,1},{65... | collective-permute-start | bytes 282632 | tf_op jit(solution)/shard_map/ppermute | solution.py:499
  250.7 19.6 %collective-permute-start.5 = (bf16[92,4,128]{2,1,0:T(4,128)(2,1)}, bf16[92,4,128]{2,1,0:T(4,128)(2,1)S(1)}, u32[]{:S(2)}, u32[]{:S(2)}) collective-permute-start(bf16[92,4,128]{2,1,0:T(4,128)(2,1)} %get-tuple-element.15.own), channel_id=1, source_target_pairs={{0,1},{1,2},{2,3},{3,4},{4,5},{5,6},{6,7},{7,0},{8,9},{9,10},{10,1... | collective-permute-start | bytes 282632 | tf_op jit(solution)/shard_map/ppermute | solution.py:498
  251.7 18.7 %collective-permute-start.4 = (bf16[92,4,128]{2,1,0:T(4,128)(2,1)}, bf16[92,4,128]{2,1,0:T(4,128)(2,1)S(1)}, u32[]{:S(2)}, u32[]{:S(2)}) collective-permute-start(bf16[92,4,128]{2,1,0:T(4,128)(2,1)} %get-tuple-element.15.own), channel_id=1, source_target_pairs={{0,64},{64,0},{1,65},{65,1},{2,66},{66,2},{3,67},{67,3},{4,68},{68... | collective-permute-start | bytes 282632 | tf_op jit(solution)/shard_map/ppermute | solution.py:497
  270.3 0.6 copy-start.2
  270.3 0.7 copy-start.3
  270.4 0.7 copy-start.4
  270.4 0.7 copy-start.5
  270.4 0.7 copy-start.6

commit v2 on v0

v2 whole, which is shorter than its diff:
```python
import math

import jax
import jax.numpy as jnp
import ml_dtypes
import numpy as np
from jax import lax
from jax.experimental import pallas as pl
from jax.experimental.pallas import tpu as pltpu
from jax.sharding import PartitionSpec as P

NLAT = 720
NLON = 1024
KMODES = 384
LDEG = 384
ROWS = 90
COLS = 128
CH = 128
OWNERS = 64
SENT = 360
BACK = 368
PITCH = CH + 1
F32 = jnp.float32
BF16 = jnp.bfloat16
MIB = 1024 * 1024
GELU_ONE = math.sqrt(2.0 / math.pi)
GELU_THREE = 0.044715 * GELU_ONE


def make_tables(nlat, nlon, kmodes, ldeg):
    column = np.arange(nlon, dtype=np.int64)[:, None]
    wavenum = np.arange(kmodes, dtype=np.int64)[None, :]
    step = np.float32(2.0 * math.pi / nlon)
    phase_cos = (column * wavenum % nlon).astype(np.float32) * step
    phase_sin = (column * (wavenum + 1) % nlon).astype(np.float32) * step
    lon_table = np.concatenate([np.cos(phase_cos), np.sin(phase_sin)], axis=1)
    lon_table = lon_table * np.float32(math.sqrt(2.0 / nlon))
    latrow = np.arange(nlat, dtype=np.int64)[:, None]
    degree = np.arange(ldeg, dtype=np.int64)[None, :]
    phase_lat = (degree * (2 * latrow + 1) % (4 * nlat)).astype(np.float32) * np.float32(
        math.pi / (2 * nlat)
    )
    lat_table = np.cos(phase_lat) * np.float32(math.sqrt(2.0 / nlat))
    return (lon_table.astype(ml_dtypes.bfloat16), lat_table.astype(ml_dtypes.bfloat16))


def arrange_lon(lon_table):
    cosines = np.arange(KMODES)
    sines = np.arange(1, KMODES + 1)
    place = np.concatenate([cosines, sines])
    zero = lon_table[:256, place % 4 == 0]
    two = lon_table[:256, place % 4 == 2]
    odd = lon_table[:512, place % 2 == 1]
    blank = np.zeros((256, 64), lon_table.dtype)
    return (
        np.concatenate([zero, blank], axis=1),
        np.concatenate([blank, two], axis=1),
        odd,
    )


def arrange_lat(lat_table):
    blocks = lat_table.reshape(4, 2, ROWS, LDEG)
    main = blocks[:, :, :80].reshape(4, 160, LDEG)
    middle = blocks[:, :, 80:88].reshape(4, 16, LDEG)
    last = blocks[:, :, 88:90]
    made = []
    for m in range(4):
        tail = np.zeros((4, 2, 4, 2, LDEG), lat_table.dtype)
        tail[:, :, m] = last
        tail = tail.reshape(4, 16, LDEG)
        made.append(np.concatenate([main, middle, tail], axis=1).reshape(768, LDEG))
    return np.stack(made)


def pack_kernel(
    atmos,
    cotangent,
    ocean,
    mask,
    coupling,
    conv,
    head,
    out,
    weights,
    below,
    above,
    in_a,
    in_c,
    warm,
    sea_cells,
    gains,
    decoder,
    held_a,
    held_c,
    last,
    sems,
):
    def fetches(i, rows):
        span = pl.ds(16 * i, rows)
        return [
            pltpu.make_async_copy(atmos.at[span], in_a.at[span], sems.at[0, i]),
            pltpu.make_async_copy(cotangent.at[span], in_c.at[span], sems.at[1, i]),
        ]

    surface = [
        pltpu.make_async_copy(ocean.at[:, pl.ds(0, 16), :], warm, sems.at[2, 0]),
        pltpu.make_async_copy(mask, sea_cells, sems.at[2, 1]),
        pltpu.make_async_copy(coupling, gains, sems.at[2, 2]),
    ]
    others = [
        pltpu.make_async_copy(conv, weights.at[pl.ds(0, 720)], sems.at[2, 3]),
        pltpu.make_async_copy(head, decoder, sems.at[2, 4]),
        pltpu.make_async_copy(ocean.at[pl.ds(ROWS - 1, 1)], below, sems.at[2, 5]),
        pltpu.make_async_copy(ocean.at[pl.ds(0, 1)], above, sems.at[3, 0]),
    ]
    for copy in surface:
        copy.start()
    for i in range(6):
        for copy in fetches(i, 16 if i < 5 else 10):
            copy.start()
    for copy in others:
        copy.start()
    for copy in surface:
        copy.wait()
    gain = jnp.broadcast_to(gains[...], (CH, COLS)).T

    def widen(i, rows):
        for copy in fetches(i, rows):
            copy.wait()
        for r in range(rows):
            row = 16 * i + r
            sea = sea_cells[pl.ds(row, 1), :].astype(F32)
            forcing = sea * warm[row].astype(F32)[0:1]
            held_a[r * PITCH : r * PITCH + CH, :] = in_a[row].astype(F32) + forcing * gain
            held_c[r * PITCH : r * PITCH + CH, :] = in_c[row].astype(F32)

    @pl.loop(0, 5)
    def _(i):
        widen(i, 16)
        base = pl.multiple_of(64 * i, 64)
        for ch in range(CH):
            for f, held in enumerate((held_a, held_c)):
                at = base + 32 * f + 16 * (ch % 2)
                out[ch // 2, pl.ds(at, 16), :] = held[pl.ds(ch, 16, stride=PITCH), :].astype(BF16)

    widen(5, 10)
    for d in range(OWNERS):
        for f, held in enumerate((held_a, held_c)):
            pair = [held[pl.ds(2 * d + c, 8, stride=PITCH), :] for c in range(2)]
            out[d, 320 + 16 * f : 336 + 16 * f, :] = jnp.concatenate(pair, axis=0).astype(BF16)
            for t in range(2):
                both = held[(8 + t) * PITCH + 2 * d : (8 + t) * PITCH + 2 * d + 2, :]
                for c in range(2):
                    row = 4 * f + 2 * c + t
                    last[d, row : row + 1, :] = both[c : c + 1]
        out[d, 352:360, :] = last[d].astype(BF16)

    for copy in others:
        copy.wait()
    weights[720:800, :] = jnp.concatenate(
        [decoder[...].astype(F32), jnp.zeros((4, 128), F32)], axis=0
    ).astype(BF16)


def vmem():
    return pl.BlockSpec(memory_space=pltpu.VMEM)


def near(array):
    return pltpu.with_memory_space_constraint(array, pltpu.VMEM)


def in_hbm():
    return pl.BlockSpec(memory_space=pltpu.HBM)


def pack(atmos, cotangent, ocean, sea_mask, coupling, conv, head):
    given = (atmos, cotangent, ocean, sea_mask, coupling[None, :], conv, head)
    return pl.pallas_call(
        pack_kernel,
        in_specs=[in_hbm()] * 7,
        out_specs=[vmem()] * 4,
        out_shape=[
            pltpu.VMEM((OWNERS, SENT, COLS), BF16),
            pltpu.VMEM((800, 128), BF16),
            pltpu.VMEM((1, 76, COLS), BF16),
            pltpu.VMEM((1, 76, COLS), BF16),
        ],
        scratch_shapes=[
            pltpu.VMEM((ROWS, CH, COLS), BF16),
            pltpu.VMEM((ROWS, CH, COLS), BF16),
            pltpu.VMEM((ROWS, 16, COLS), BF16),
            pltpu.VMEM((ROWS, COLS), jnp.int32),
            pltpu.VMEM((1, CH), F32),
            pltpu.VMEM((76, 128), BF16),
            pltpu.VMEM((16 * PITCH, COLS), F32),
            pltpu.VMEM((16 * PITCH, COLS), F32),
            pltpu.VMEM((OWNERS, 8, COLS), F32),
            pltpu.SemaphoreType.DMA((4, 6)),
        ],
        compiler_params=pltpu.CompilerParams(vmem_limit_bytes=14 * MIB),
        name="pack",
    )(*[pltpu.with_memory_space_constraint(array, pltpu.HBM) for array in given])


def spectral_kernel(
    got,
    lon_zero,
    lon_two,
    lon_odd,
    back_zero,
    back_two,
    back_odd,
    lat,
    lat_back,
    weight,
    out,
    grad,
    coef,
    kept,
    back,
    edge_in,
    edge,
    halo,
):
    edge_in[...] = jnp.zeros_like(edge_in)
    edge[...] = jnp.zeros_like(edge)

    def dot(one, two):
        return jnp.dot(one, two, preferred_element_type=F32)

    @pl.loop(0, 4)
    def _(p):
        found = []
        for a in range(2):
            first = 16 * p + 8 * a
            quarter = [
                jnp.concatenate([got[first + 2 * q + h].astype(F32) for h in range(2)], axis=1)
                for q in range(4)
            ]
            even_0 = quarter[0] + quarter[2]
            even_1 = quarter[1] + quarter[3]
            odd = jnp.concatenate(
                [(quarter[0] - quarter[2]).astype(BF16), (quarter[1] - quarter[3]).astype(BF16)],
                axis=1,
            )
            zero = dot((even_0 + even_1).astype(BF16), lon_zero[...])
            two = dot((even_0 - even_1).astype(BF16), lon_two[...])
            found.append(
                [
                    zero[:, 0:128],
                    zero[:, 128:256] + two[:, 0:128],
                    two[:, 128:256],
                    dot(odd, lon_odd[...]),
                ]
            )
        for n, cols in enumerate(
            (slice(0, 128), slice(128, 256), slice(256, 384), slice(384, 768))
        ):
            for m in range(4):
                for a in range(2):
                    for i in range(5):
                        coef[m, p, 80 * a + 16 * i : 80 * a + 16 * i + 16, cols] = found[a][n][
                            64 * i + 16 * m : 64 * i + 16 * m + 16
                        ].astype(BF16)
                coef[m, p, 160:176, cols] = jnp.concatenate(
                    [found[a][n][320 + 8 * m : 328 + 8 * m] for a in range(2)], axis=0
                ).astype(BF16)
                coef[m, p, 176:192, cols] = jnp.concatenate(
                    [found[a][n][352:360] for a in range(2)], axis=0
                ).astype(BF16)
        for a in range(2):
            block = 2 * p + a
            for o in range(8):
                lanes = slice(128 * o, 128 * o + 128)
                low = got[8 * block + o, 352:360, :].astype(F32)
                for c in range(2):
                    high = got[8 * block + o, 16 * c : 16 * c + 16, :].astype(F32)
                    edge_in[block + 2, c : c + 1, lanes] = low[2 * c + 1 : 2 * c + 2]
                    edge_in[block, 2 + c : 3 + c, lanes] = high[0:1]

    for c in range(2):
        scale = jnp.broadcast_to(weight[c : c + 1, :], (256, LDEG)).T
        total = jnp.zeros((LDEG, 128), F32)
        for n in range(3):
            cols = slice(256 * n, 256 * n + 256)
            spectra = []
            for f in range(2):
                m = 2 * f + c
                found = dot(lat[m], coef[m, :, :, cols].reshape(768, 256))
                kept[m, :, cols] = (found * scale).astype(BF16)
                spectra.append(found)
            product = spectra[0] * spectra[1]
            total = total + product[:, :128] + product[:, 128:]
        grad[c : c + 1, :] = jnp.sum(total.T, axis=0, keepdims=True) / KMODES
    for n in range(3):
        cols = slice(256 * n, 256 * n + 256)
        tails = [jnp.zeros((16, 256), F32) for _ in range(4)]
        for m in range(4):
            found = dot(lat_back[m], kept[m, :, cols])
            for p in range(4):
                base = 192 * p
                back[p, 160 * m : 160 * m + 160, cols] = found[base : base + 160].astype(BF16)
                back[p, 640 + 16 * m : 656 + 16 * m, cols] = found[
                    base + 160 : base + 176
                ].astype(BF16)
                tail = found[base + 176 : base + 192]
                tails[p] = tails[p] + tail
                if m < 2:
                    for a in range(2):
                        block = 2 * p + a
                        row = 8 * a + 2 * m + 1
                        edge[block + 2, m : m + 1, cols] = tail[row : row + 1]
                        edge[block, 2 + m : 3 + m, cols] = found[base + 80 * a : base + 80 * a + 1]
        for p in range(4):
            back[p, 704:720, cols] = tails[p].astype(BF16)

    def inverse(rows):
        zero = dot(rows[:, 0:256], back_zero[...])
        two = dot(rows[:, 128:384], back_two[...])
        for n in range(2):
            even = zero + two if n == 0 else zero - two
            odd = dot(rows[:, 384:768], back_odd[:, 256 * n : 256 * n + 256])
            yield 2 * n, even + odd
            yield 2 * n + 4, even - odd

    for o, found in inverse(edge[1:9].reshape(64, 768).astype(BF16)):
        lanes = slice(128 * o, 128 * o + 256)
        halo[:, :, lanes] = found.reshape(8, 8, 256) + edge_in[1:9, :, lanes]

    @pl.loop(0, 4)
    def _(p):
        for first, found in inverse(back[p]):
            for half in range(2):
                o = first + half
                lanes = slice(128 * half, 128 * half + 128)
                for a in range(2):
                    d = 16 * p + 8 * a + o
                    for i in range(5):
                        for m in range(4):
                            at = 160 * m + 80 * a + 16 * i
                            to = 64 * i + 16 * m
                            out[d, to : to + 16, :] = (
                                found[at : at + 16, lanes] + got[d, to : to + 16, :].astype(F32)
                            ).astype(BF16)
                    for f in range(2):
                        at = 640 + 32 * f + 8 * a
                        to = 320 + 16 * f
                        pair = jnp.concatenate(
                            [found[at : at + 8, lanes], found[at + 16 : at + 24, lanes]], axis=0
                        )
                        out[d, to : to + 16, :] = (
                            pair + got[d, to : to + 16, :].astype(F32)
                        ).astype(BF16)
                    at = 704 + 8 * a
                    low = found[at : at + 8, lanes] + got[d, 352:360, :].astype(F32)
                    beyond = halo[2 * p + a, :, 128 * o : 128 * o + 128]
                    out[d, 352:368, :] = jnp.concatenate([low, beyond], axis=0).astype(BF16)


def spectral(got, lon, lat, weight):
    tables = list(lon) + [table.T for table in lon] + [lat.transpose(0, 2, 1), lat]
    return pl.pallas_call(
        spectral_kernel,
        in_specs=[vmem()] * 10,
        out_specs=[vmem(), vmem()],
        out_shape=[
            pltpu.VMEM((OWNERS, BACK, COLS), BF16),
            jax.ShapeDtypeStruct((2, LDEG), F32),
        ],
        scratch_shapes=[
            pltpu.VMEM((4, 4, 192, 768), BF16),
            pltpu.VMEM((4, LDEG, 768), BF16),
            pltpu.VMEM((4, 720, 768), BF16),
            pltpu.VMEM((10, 8, NLON), F32),
            pltpu.VMEM((10, 8, 768), F32),
            pltpu.VMEM((8, 8, NLON), F32),
        ],
        compiler_params=pltpu.CompilerParams(vmem_limit_bytes=20 * MIB),
        name="spectral",
    )(near(got), *[near(jnp.asarray(np.ascontiguousarray(table))) for table in tables], weight)


def spread(sent_back, i, field, held):
    base = pl.multiple_of(64 * i, 64) + 32 * field
    for ch in range(CH):
        at = base + 16 * (ch % 2)
        held[pl.ds(ch, 16, stride=PITCH), :] = sent_back[ch // 2, pl.ds(at, 16), :].astype(F32)


def spread_last(sent_back, field, held):
    for d in range(OWNERS):
        near = sent_back[d, 320 + 16 * field : 336 + 16 * field, :].astype(F32)
        last = sent_back[d, 352:368, :].astype(F32)
        for c in range(2):
            held[pl.ds(2 * d + c, 8, stride=PITCH), :] = near[8 * c : 8 * c + 8]
            for t in range(2):
                row = 4 * field + 2 * c + t
                at = (8 + t) * PITCH + 2 * d + c
                held[at : at + 1, :] = last[row : row + 1]


def unpack_rows(sent_back, field, out, held, staged, sems, visit):
    def send(i, rows):
        span = pl.ds(16 * i, rows)
        return pltpu.make_async_copy(staged.at[span], out.at[span], sems.at[i])

    @pl.loop(0, 5)
    def _(i):
        spread(sent_back, i, field, held)
        for r in range(16):
            staged[16 * i + r] = held[r * PITCH : r * PITCH + CH, :].astype(BF16)
            visit(16 * i + r)
        send(i, 16).start()

    spread_last(sent_back, field, held)
    for r in range(10):
        staged[80 + r] = held[r * PITCH : r * PITCH + CH, :].astype(BF16)
        visit(80 + r)
    send(5, 10).start()

    def finish():
        for i in range(6):
            send(i, 16 if i < 5 else 10).wait()

    return finish


def unpack_flux_kernel(
    sent_back,
    weight,
    ocean,
    top,
    bottom,
    out,
    flux,
    to_east,
    to_west,
    held,
    staged,
    outside,
    found,
    sems,
):
    def put(row, cells):
        sums = jnp.dot(weight[...], cells, preferred_element_type=F32)
        found[pl.ds(4 * row, 4), :] = sums[0:4]

    finish = unpack_rows(
        sent_back, 0, out, held, staged, sems, lambda row: put(row + 1, staged[row])
    )
    for d in range(OWNERS):
        beyond = sent_back[d, 352:368, :].astype(F32)
        for side in range(2):
            outside[side, 2 * d : 2 * d + 2, :] = beyond[8 + 2 * side : 10 + 2 * side]
    put(0, outside[0].astype(BF16))
    put(91, outside[1].astype(BF16))

    lane = lax.broadcasted_iota(jnp.int32, (76, COLS), 1)

    def gather(row, cells, kept):
        at = lane == row
        return (
            jnp.where(at, pltpu.roll(cells, lax.rem(row + 1, COLS), 1), kept[0]),
            jnp.where(at, pltpu.roll(cells, row, 1), kept[1]),
        )

    blank = jnp.zeros((76, COLS), BF16)
    edges = gather(jnp.int32(0), top[0], (blank, blank))
    edges = gather(jnp.int32(91), bottom[0], edges)
    edges = lax.fori_loop(
        0, ROWS, lambda row, kept: gather(row + 1, ocean[row], kept), edges, unroll=18
    )

    sums = found[...].astype(BF16)
    flux[...] = sums
    for side, message in enumerate((to_east, to_west)):
        message[0:368, :] = sums
        message[368:448, :] = jnp.concatenate(
            [edges[side].astype(F32), jnp.zeros((4, COLS), F32)], axis=0
        ).astype(BF16)
    finish()


def unpack_taps_kernel(
    sent_back,
    weights,
    weights_other,
    ocean,
    top,
    bottom,
    out,
    taps,
    conv,
    head,
    held,
    staged,
    sems,
):
    finish = unpack_rows(sent_back, 1, out, held, staged, sems, lambda row: None)

    for half, given in enumerate((weights, weights_other)):
        rows = slice(128 * half, 128 * half + 128)
        wide = jnp.concatenate([given[0:720, :].astype(F32), jnp.zeros((48, 128), F32)], axis=0)
        conv[rows, :] = wide.T.astype(BF16)
        head[:, rows] = given[720:800, :]

    def build(row, cells):
        wide = jnp.concatenate([cells, jnp.zeros((4, COLS), BF16)], axis=0)
        base = pl.multiple_of(240 * row, 16)
        taps[pl.ds(base, 80), :] = pltpu.roll(wide, 1, 1)
        taps[pl.ds(base + 80, 80), :] = wide
        taps[pl.ds(base + 160, 80), :] = pltpu.roll(wide, COLS - 1, 1)

    build(0, top[0])
    build(91, bottom[0])
    taps[92 * 240 :, :] = jnp.zeros((48, COLS), BF16)

    @pl.loop(0, ROWS, unroll=18)
    def _(row):
        build(row + 1, ocean[row])

    finish()


def unpack_scratch():
    return [pltpu.VMEM((16 * PITCH, COLS), F32), pltpu.VMEM((ROWS, CH, COLS), BF16)]


def unpack_flux(sent_back, weight, ocean, top, bottom):
    return pl.pallas_call(
        unpack_flux_kernel,
        in_specs=[vmem()] * 5,
        out_specs=[in_hbm(), vmem(), vmem(), vmem()],
        out_shape=[
            jax.ShapeDtypeStruct((ROWS, CH, COLS), BF16),
            jax.ShapeDtypeStruct((368, COLS), BF16),
            jax.ShapeDtypeStruct((448, COLS), BF16),
            jax.ShapeDtypeStruct((448, COLS), BF16),
        ],
        scratch_shapes=unpack_scratch()
        + [
            pltpu.VMEM((2, CH, COLS), F32),
            pltpu.VMEM((368, COLS), F32),
            pltpu.SemaphoreType.DMA((6,)),
        ],
        compiler_params=pltpu.CompilerParams(vmem_limit_bytes=12 * MIB),
        name="unpack_flux",
    )(near(sent_back), weight, near(ocean), top, bottom)


def unpack_taps(sent_back, weights, weights_other, ocean, top, bottom):
    return pl.pallas_call(
        unpack_taps_kernel,
        in_specs=[vmem()] * 6,
        out_specs=[in_hbm(), vmem(), vmem(), vmem()],
        out_shape=[
            jax.ShapeDtypeStruct((ROWS, CH, COLS), BF16),
            pltpu.VMEM((92 * 240 + 48, COLS), BF16),
            pltpu.VMEM((256, 768), BF16),
            pltpu.VMEM((80, 256), BF16),
        ],
        scratch_shapes=unpack_scratch() + [pltpu.SemaphoreType.DMA((6,))],
        compiler_params=pltpu.CompilerParams(vmem_limit_bytes=12 * MIB),
        cost_estimate=pl.CostEstimate(flops=0, bytes_accessed=12_000_000, transcendentals=0),
        name="unpack_taps",
    )(near(sent_back), weights, weights_other, near(ocean), top, bottom)


def ocean_kernel(
    own,
    other,
    left,
    left_other,
    right,
    right_other,
    unfinished,
    conv,
    head,
    ocean,
    mask,
    out,
    taps,
    fluxes,
    hidden,
    staged,
    sems,
):
    def whole(one, two):
        total = one[0:368, :].astype(F32) + two[...].astype(F32)
        return total.astype(BF16).astype(F32)

    column = lax.broadcasted_iota(jnp.int32, (368, COLS), 1)
    middle = whole(own, other)
    west = pltpu.roll(whole(left, left_other), 1, 1)
    east = pltpu.roll(whole(right, right_other), COLS - 1, 1)
    fluxes[0] = jnp.where(column == 0, west, pltpu.roll(middle, 1, 1))
    fluxes[1] = middle
    fluxes[2] = jnp.where(column == COLS - 1, east, pltpu.roll(middle, COLS - 1, 1))

    lane = lax.broadcasted_iota(jnp.int32, (80, COLS), 1)
    first_edge = left[368:448, :]
    final_edge = right[368:448, :]

    taps[92 * 240 :, :] = jnp.zeros((48, COLS), BF16)

    @pl.loop(0, ROWS + 2, unroll=23)
    def _(row):
        base = pl.multiple_of(240 * row, 16)
        first = pltpu.roll(first_edge, lax.rem(COLS - row, COLS), 1)
        final = pltpu.roll(final_edge, COLS - 1 - row, 1)
        shifts = (
            jnp.where(lane == 0, first, unfinished[pl.ds(base, 80), :]),
            unfinished[pl.ds(base + 80, 80), :],
            jnp.where(lane == COLS - 1, final, unfinished[pl.ds(base + 160, 80), :]),
        )
        for b, cells in enumerate(shifts):
            at = base + 80 * b
            taps[pl.ds(at, 64), :] = cells[0:64]
            rest = [cells[64:80].astype(F32)[0:12], fluxes[b, pl.ds(4 * row, 4), :]]
            taps[pl.ds(at + 64, 16), :] = jnp.concatenate(rest, axis=0).astype(BF16)

    def send(g):
        span = pl.ds(10 * g, 10)
        return pltpu.make_async_copy(staged.at[span], out.at[span], sems.at[g])

    def window(row):
        return taps[pl.ds(pl.multiple_of(240 * row, 16), 768), :]

    def convolve(g):
        for pair in range(5):
            first = 10 * g + 2 * pair
            around = jnp.concatenate([window(first), window(first + 1)], axis=1)
            x = jnp.dot(conv[...], around, preferred_element_type=F32)
            bent = jnp.tanh(x * (GELU_ONE + GELU_THREE * (x * x)))
            half = 0.5 * x
            hidden[lax.rem(g, 2), :, 256 * pair : 256 * pair + 256] = (half + half * bent).astype(
                BF16
            )

    def decode(g):
        delta = jnp.dot(head[...], hidden[lax.rem(g, 2)], preferred_element_type=F32)
        for k in range(10):
            row = 10 * g + k
            sea = mask[pl.ds(row, 1), :].astype(F32)
            staged[row] = (
                ocean[row].astype(F32) + sea * delta[0:76, COLS * k : COLS * k + COLS]
            ).astype(BF16)
        send(g).start()

    convolve(jnp.int32(0))

    @pl.loop(1, 9)
    def _(g):
        convolve(g)
        decode(g - 1)

    decode(jnp.int32(8))
    for g in range(9):
        send(g).wait()


def ocean_step(fluxes, taps, conv, head, ocean, sea_mask):
    return pl.pallas_call(
        ocean_kernel,
        in_specs=[vmem()] * 11,
        out_specs=in_hbm(),
        out_shape=jax.ShapeDtypeStruct((ROWS, 76, COLS), BF16),
        scratch_shapes=[
            pltpu.VMEM((92 * 240 + 48, COLS), BF16),
            pltpu.VMEM((3, 368, COLS), F32),
            pltpu.VMEM((2, 256, 1280), BF16),
            pltpu.VMEM((ROWS, 76, COLS), BF16),
            pltpu.SemaphoreType.DMA((9,)),
        ],
        compiler_params=pltpu.CompilerParams(vmem_limit_bytes=14 * MIB),
        name="ocean",
    )(*fluxes, near(taps), near(conv), near(head), near(ocean), sea_mask)


def after(value, *others):
    return lax.optimization_barrier((value,) + others)[0]


def local(
    atmos,
    cotangent,
    ocean,
    sea_mask,
    spectral_weight,
    coupling,
    flux_weight,
    conv_weight,
    head_weight,
):
    atmos = atmos.transpose(1, 0, 2)
    cotangent = cotangent.transpose(1, 0, 2)
    ocean = ocean.transpose(1, 0, 2)
    ring = range(8)
    east = [(k, (k + 1) % 8) for k in ring]
    west = [((k + 1) % 8, k) for k in ring]
    swap = [(0, 1), (1, 0)]
    lon_table, lat_table = make_tables(NLAT, NLON, KMODES, LDEG)

    sent, weights, below, above = pack(
        atmos,
        cotangent,
        ocean,
        sea_mask,
        coupling,
        conv_weight.reshape(720, 128),
        head_weight.T,
    )
    weights_other = lax.ppermute(weights, "group", swap)
    top = lax.ppermute(below, "lat", [(k, k + 1) for k in range(7)])
    bottom = lax.ppermute(above, "lat", [(k + 1, k) for k in range(7)])
    sent, weights_other, top, bottom = lax.optimization_barrier(
        (sent, weights_other, top, bottom)
    )
    got = lax.all_to_all(sent, ("lat", "lon"), split_axis=0, concat_axis=0, tiled=True)
    sent_back, grad_spectral = spectral(
        got, arrange_lon(lon_table), arrange_lat(lat_table), spectral_weight
    )
    returned = lax.all_to_all(sent_back, ("lat", "lon"), split_axis=0, concat_axis=0, tiled=True)
    atmos_next, flux, to_east, to_west = unpack_flux(returned, flux_weight, ocean, top, bottom)
    across = [(8 * g + k, 8 * (1 - g) + (k + 1) % 8) for g in range(2) for k in ring]
    counter = [(8 * g + k, 8 * (1 - g) + (k - 1) % 8) for g in range(2) for k in ring]
    fluxes = [
        flux,
        lax.ppermute(flux, "group", swap),
        lax.ppermute(to_east, "lon", east),
        lax.ppermute(flux, ("group", "lon"), across),
        lax.ppermute(to_west, "lon", west),
        lax.ppermute(flux, ("group", "lon"), counter),
    ]
    grad_atmos, taps, conv, head = unpack_taps(
        after(returned, flux), weights, weights_other, ocean, top, bottom
    )
    ocean_next = ocean_step(fluxes, taps, conv, head, ocean, sea_mask)
    return (
        atmos_next.transpose(1, 0, 2),
        grad_atmos.transpose(1, 0, 2),
        grad_spectral,
        ocean_next.transpose(1, 0, 2),
    )


def solution(mesh):
    in_specs = (
        P("group", "lat", "lon"),
        P("group", "lat", "lon"),
        P(None, "lat", "lon"),
        P("lat", "lon"),
        P(("group", "lat", "lon"), None),
        P("group"),
        P(None, "group"),
        P(None, None, None, "group"),
        P("group", None),
    )
    out_specs = (
        P("group", "lat", "lon"),
        P("group", "lat", "lon"),
        P(("group", "lat", "lon"), None),
        P(None, "lat", "lon"),
    )
    return jax.shard_map(local, mesh=mesh, in_specs=in_specs, out_specs=out_specs, check_vma=False)
```

time: 715 us -> 216 us (0.30)
  local copies, waits for them, and re-layouts: 165 us -> 0.06 us
  waiting for transfers between devices: 131 us -> 7.42 us
  blocking collectives: 250 us -> 162 us
  matrix products: 85.7 us -> 0 us
  other arithmetic: 46.6 us -> 0 us
  Pallas kernels: 0 us -> 32.7 us
  between operations: 14.7 us -> 0.98 us
    all_to_all x3 -> x2, blocking collectives: 250 us -> 162 us  [the longest x1 84.1 us: local(): lax.all_to_all(sent, ('lat', 'lon'), split_axis=0, concat_axis=0, tiled=T...]
    dot_general x12 -> x0, matrix products: 85.7 us -> none  [the longest x8 31 us: convolve(): jnp.einsum('irq,ih->hrq', window, conv_weight[row_shift, col_shift], pref...]
    psum x2 -> x0, waiting for transfers between devices: 69.8 us -> none  [the longest x1 45.6 us: local(): lax.psum(delta_part.astype(jnp.bfloat16), 'group').astype(jnp.float32)]
    all_to_all x8 -> x0, local copies, waits for them, and re-layouts: 66.1 us -> none  [the longest x2 30.2 us: local(): lax.all_to_all(lax.all_to_all(fields, 'lat', split_axis=1, concat_axis=2,...]
    all_to_all x1 -> x0, waiting for transfers between devices: 55.4 us -> none  [local(): lax.all_to_all(lax.all_to_all(fields, 'lat', split_axis=1, concat_axis=2,...]
    another operation x1 -> x0, local copies, waits for them, and re-layouts: 43.9 us -> none  [local(): fields = jnp.stack([atmos_input, cotangent])]
    convert_element_type x3 -> x0, local copies, waits for them, and re-layouts: 41.1 us -> none  [the longest x1 28.9 us: lon_inverse(): return jnp.einsum('fcak,nk->fcan', lat_back, lon_table, preferred_element...]
    pallas_call x0 -> x5, Pallas kernels: none -> 32.7 us  [the longest x1 11.8 us: spectral(): pl.pallas_call(spectral_kernel, in_specs=[vmem()] * 10, out_specs=[vmem()...]
  transfers between devices with their start and end apart: 7 -> 8, of which waited for: 5 -> 2; matrix products, arithmetic and copies ran while one was open for 4% -> 0% of each run, Pallas kernels for 0% -> 1%
where the time goes in v2:
time: 216 us
  blocking collectives  162 us (75%)
  Pallas kernels  32.7 us (15%)
  starting transfers between devices  12.4 us (6%)
  waiting for transfers between devices  7.42 us (3%)
    all_to_all x1, blocking collectives, local(): lax.all_to_all(sent, ('lat', 'lon'), split_axis=0, concat_axis=0, tiled=T...  84.1 us
    all_to_all x1, blocking collectives, local(): lax.all_to_all(sent_back, ('lat', 'lon'), split_axis=0, concat_axis=0, ti...  77.9 us
    pallas_call x1, Pallas kernels, spectral(): pl.pallas_call(spectral_kernel, in_specs=[vmem()] * 10, out_specs=[vmem()...  11.8 us
    pallas_call x1, Pallas kernels, ocean_step(): pl.pallas_call(ocean_kernel, in_specs=[vmem()] * 11, out_specs=in_hbm(),...  11.5 us
  transfers between devices with their start and end apart: 8, of which 2 were waited for; matrix products, arithmetic and copies ran while one was open for 0% of the time, Pallas kernels for 1%

profile of v2, /device:TPU:1, one launch (start us, length us, event | category | flops | bytes accessed | tf_op | source)
XLA Modules:
  0.0 215.6 jit_solution(16462415245234748690)
XLA Ops:
  0.6 3.5 %pack.1 = (bf16[64,360,128]{2,1,0:T(8,128)(2,1)S(1)}, bf16[800,128]{1,0:T(8,128)(2,1)S(1)}, bf16[1,76,128]{2,1,0:T(8,128)(2,1)S(1)}, bf16[1,76,128]{2,1,0:T(8,128)(2,1)S(1)}) custom-call(bf16[90,128,128]{2,1,0:T(8,128)(2,1)} %bitcast.13, bf16[90,128,128]{2,1,0:T(8,128)(2,1)} %bitcast.14, bf16[90,76,128]{2,1,0:T(8,128)(2,1)} %bitcast.9, s32[90,128]{1,0:T(8,128)} %mask.3, ...), custom_call_target="tpu_custom_call" | custom-call | tf_op jit(solution)/shard_map/pack/pallas_call | solution.py:180
  4.2 2.2 %collective-permute-start = (bf16[800,128]{1,0:T(8,128)(2,1)S(1)}, bf16[800,128]{1,0:T(8,128)(2,1)S(1)}, u32[]{:S(2)}, u32[]{:S(2)}) collective-permute-start(bf16[800,128]{1,0:T(8,128)(2,1)S(1)} %get-tuple-element.24.weights), channel_id=1, source_target_pairs={{0,64},{64,0},{1,65},{65,1},{2,66},{66,2},{3,67},{67,3},{4,68},{68... | collective-permute-start | bytes 614408 | tf_op jit(solution)/shard_map/ppermute | solution.py:715
  6.4 3.5 %collective-permute-start.1 = (bf16[1,76,128]{2,1,0:T(8,128)(2,1)S(1)}, bf16[1,76,128]{2,1,0:T(8,128)(2,1)S(1)}, u32[]{:S(2)}, u32[]{:S(2)}) collective-permute-start(bf16[1,76,128]{2,1,0:T(8,128)(2,1)S(1)} %get-tuple-element.25), channel_id=1, source_target_pairs={{0,8},{8,16},{16,24},{24,32},{32,40},{40,48},{48,56},{1,9},{9,17},... | collective-permute-start | bytes 58376 | tf_op jit(solution)/shard_map/ppermute | solution.py:716
  9.9 1.3 collective-permute-start.2
  11.2 0.0 collective-permute-done.1.top
  11.2 3.4 %collective-permute-done.2.bottom = bf16[1,76,128]{2,1,0:T(8,128)(2,1)S(1)} collective-permute-done((bf16[1,76,128]{2,1,0:T(8,128)(2,1)S(1)}, bf16[1,76,128]{2,1,0:T(8,128)(2,1)S(1)}, u32[]{:S(2)}, u32[]{:S(2)}) %collective-permute-start.2) | collective-permute-done | bytes 19488 | tf_op jit(solution)/shard_map/ppermute | solution.py:717
  14.6 0.0 collective-permute-done.weights_other
  14.6 0.0 copy-start.1
  14.6 0.0 copy-start.2
  14.6 0.0 copy-start.3
  14.6 0.0 copy-start.4
  14.7 0.0 copy-start.6
  14.7 0.0 copy-start.7
  14.7 0.0 copy-start.8
  14.7 0.0 copy-start.9
  14.7 0.0 copy-start.10
  14.7 84.1 %all_to_all.10.got = bf16[64,360,128]{2,1,0:T(8,128)(2,1)S(1)} all-to-all(bf16[64,360,128]{2,1,0:T(8,128)(2,1)S(1)} %get-tuple-element.27), channel_id=1, replica_groups=mesh['group'=2,'lat'=8,'lon'=8] {'lat','lon'}, dimensions={0} | all-to-all | bytes 11796480 | tf_op jit(solution)/shard_map/all_to_all | solution.py:721
  98.8 0.0 copy-done.1
  98.8 0.0 copy-done.2
  98.8 0.0 copy-done.3
  98.8 0.0 copy-done.4
  98.8 0.0 copy-done.6
  98.8 0.0 copy-done.7
  98.9 0.0 copy-done.8
  98.9 0.0 copy-done.9
  98.9 0.0 copy-done.10
  98.9 11.8 %spectral.1 = (bf16[64,368,128]{2,1,0:T(8,128)(2,1)S(1)}, f32[2,384]{1,0:T(2,128)}) custom-call(bf16[64,360,128]{2,1,0:T(8,128)(2,1)S(1)} %all_to_all.10.got, bf16[256,256]{1,0:T(8,128)(2,1)S(1)} %copy-done.6, bf16[256,256]{1,0:T(8,128)(2,1)S(1)} %copy-done.7, bf16[512,384]{1,0:T(8,128)(2,1)S(1)} %copy-done.3, bf16[256,256]{1,0:T(8,128)(2,1)S(1)} %copy-done.8, ...), custom_call_target="tpu_custom_call" | custom-call | tf_op jit(solution)/shard_map/spectral/pallas_call | solution.py:364
  110.7 0.0 copy-start
  110.7 0.0 copy-start.11
  110.7 77.9 %all_to_all.11.sent_back = bf16[64,368,128]{2,1,0:T(8,128)(2,1)S(1)} all-to-all(bf16[64,368,128]{2,1,0:T(8,128)(2,1)S(1)} %get-tuple-element.28), channel_id=1, replica_groups=mesh['group'=2,'lat'=8,'lon'=8] {'lat','lon'}, dimensions={0} | all-to-all | bytes 12058624 | tf_op jit(solution)/shard_map/all_to_all | solution.py:725
  188.6 0.0 copy-done
  188.6 0.0 copy-done.11
  188.6 3.6 %unpack_flux.1 = (bf16[90,128,128]{2,1,0:T(8,128)(2,1)}, bf16[368,128]{1,0:T(8,128)(2,1)S(1)}, bf16[448,128]{1,0:T(8,128)(2,1)S(1)}, bf16[448,128]{1,0:T(8,128)(2,1)S(1)}) custom-call(bf16[64,368,128]{2,1,0:T(8,128)(2,1)S(1)} %all_to_all.11.sent_back, bf16[4,128]{1,0:T(4,128)(2,1)S(1)} %copy-done.11, bf16[90,76,128]{2,1,0:T(8,128)(2,1)S(1)} %bitcast.10, ...), custom_call_target="tpu_custom_call" | custom-call | tf_op jit(solution)/shard_map/unpack_flux/pallas_call | solution.py:532
  192.3 1.4 collective-permute-start.4
  193.6 0.0 collective-permute-start.6
  193.6 0.0 copy-start.5
  193.6 1.2 collective-permute-start.3
  194.9 2.0 collective-permute-start.5
  196.8 0.8 collective-permute-start.7
  197.7 2.3 %unpack_taps.1 = (bf16[90,128,128]{2,1,0:T(8,128)(2,1)}, bf16[22128,128]{1,0:T(8,128)(2,1)S(1)}, bf16[256,768]{1,0:T(8,128)(2,1)S(1)}, bf16[80,256]{1,0:T(8,128)(2,1)S(1)}) custom-call(bf16[64,368,128]{2,1,0:T(8,128)(2,1)S(1)} %all_to_all.11.sent_back, bf16[800,128]{1,0:T(8,128)(2,1)S(1)} %get-tuple-element.24.weights, ...), custom_call_target="tpu_custom_call" | custom-call | bytes 12000000 | tf_op jit(solution)/shard_map/unpack_taps/pallas_call | solution.py:554
  199.9 0.0 collective-permute-done.3.other
  199.9 4.0 %collective-permute-done.5.left_other = bf16[368,128]{1,0:T(8,128)(2,1)S(1)} collective-permute-done((bf16[368,128]{1,0:T(8,128)(2,1)S(1)}, bf16[368,128]{1,0:T(8,128)(2,1)S(1)}, u32[]{:S(2)}, u32[]{:S(2)}) %collective-permute-start.5) | collective-permute-done | bytes 94240 | tf_op jit(solution)/shard_map/ppermute | solution.py:733
  204.0 0.0 collective-permute-done.7.right_other
  204.0 0.0 collective-permute-done.4.left
  204.0 0.0 collective-permute-done.6.right
  204.0 0.0 copy-done.5
  204.0 11.5 %ocean.1 = bf16[90,76,128]{2,1,0:T(8,128)(2,1)} custom-call(bf16[368,128]{1,0:T(8,128)(2,1)S(1)} %get-tuple-element.32.own, bf16[368,128]{1,0:T(8,128)(2,1)S(1)} %collective-permute-done.3.other, bf16[448,128]{1,0:T(8,128)(2,1)S(1)} %collective-permute-done.4.left, bf16[368,128]{1,0:T(8,128)(2,1)S(1)} %collective-permute-done.5.left_other, ...), custom_call_target="tpu_custom_call" | custom-call | tf_op jit(solution)/shard_map/ocean/pallas_call | solution.py:665
Async XLA Ops:
  4.2 10.5 %collective-permute-start = (bf16[800,128]{1,0:T(8,128)(2,1)S(1)}, bf16[800,128]{1,0:T(8,128)(2,1)S(1)}, u32[]{:S(2)}, u32[]{:S(2)}) collective-permute-start(bf16[800,128]{1,0:T(8,128)(2,1)S(1)} %get-tuple-element.24.weights), channel_id=1, source_target_pairs={{0,64},{64,0},{1,65},{65,1},{2,66},{66,2},{3,67},{67,3},{4,68},{68... | collective-permute-start | bytes 614408 | tf_op jit(solution)/shard_map/ppermute | solution.py:715
  6.4 4.8 %collective-permute-start.1 = (bf16[1,76,128]{2,1,0:T(8,128)(2,1)S(1)}, bf16[1,76,128]{2,1,0:T(8,128)(2,1)S(1)}, u32[]{:S(2)}, u32[]{:S(2)}) collective-permute-start(bf16[1,76,128]{2,1,0:T(8,128)(2,1)S(1)} %get-tuple-element.25), channel_id=1, source_target_pairs={{0,8},{8,16},{16,24},{24,32},{32,40},{40,48},{48,56},{1,9},{9,17},... | collective-permute-start | bytes 58376 | tf_op jit(solution)/shard_map/ppermute | solution.py:716
  9.9 4.7 %collective-permute-start.2 = (bf16[1,76,128]{2,1,0:T(8,128)(2,1)S(1)}, bf16[1,76,128]{2,1,0:T(8,128)(2,1)S(1)}, u32[]{:S(2)}, u32[]{:S(2)}) collective-permute-start(bf16[1,76,128]{2,1,0:T(8,128)(2,1)S(1)} %get-tuple-element.26), channel_id=1, source_target_pairs={{8,0},{16,8},{24,16},{32,24},{40,32},{48,40},{56,48},{9,1},{17,9},... | collective-permute-start | bytes 58376 | tf_op jit(solution)/shard_map/ppermute | solution.py:717
  14.6 84.2 %copy-start.1 = (bf16[4,384,768]{2,1,0:T(8,128)(2,1)S(1)}, bf16[4,384,768]{2,1,0:T(8,128)(2,1)}, u32[]{:S(2)}) copy-start(bf16[4,384,768]{2,1,0:T(8,128)(2,1)} %constant.22.clone.lat) | copy-start | bytes 7077892
  14.6 84.2 %copy-start.2 = (bf16[4,768,384]{2,1,0:T(8,128)(2,1)S(1)}, bf16[4,768,384]{2,1,0:T(8,128)(2,1)}, u32[]{:S(2)}) copy-start(bf16[4,768,384]{2,1,0:T(8,128)(2,1)} %constant.23.clone.lat_back) | copy-start | bytes 7077892
  14.6 84.2 %copy-start.3 = (bf16[512,384]{1,0:T(8,128)(2,1)S(1)}, bf16[512,384]{1,0:T(8,128)(2,1)}, u32[]{:S(2)}) copy-start(bf16[512,384]{1,0:T(8,128)(2,1)} %constant.18.clone.lon_odd) | copy-start | bytes 1179652
  14.6 84.2 %copy-start.4 = (bf16[384,512]{1,0:T(8,128)(2,1)S(1)}, bf16[384,512]{1,0:T(8,128)(2,1)}, u32[]{:S(2)}) copy-start(bf16[384,512]{1,0:T(8,128)(2,1)} %constant.21.clone.back_odd) | copy-start | bytes 1179652
  14.7 84.2 %copy-start.6 = (bf16[256,256]{1,0:T(8,128)(2,1)S(1)}, bf16[256,256]{1,0:T(8,128)(2,1)}, u32[]{:S(2)}) copy-start(bf16[256,256]{1,0:T(8,128)(2,1)} %constant.16.clone.lon_zero) | copy-start | bytes 393220
  14.7 84.2 %copy-start.7 = (bf16[256,256]{1,0:T(8,128)(2,1)S(1)}, bf16[256,256]{1,0:T(8,128)(2,1)}, u32[]{:S(2)}) copy-start(bf16[256,256]{1,0:T(8,128)(2,1)} %constant.17.clone.lon_two) | copy-start | bytes 393220
  14.7 84.2 %copy-start.8 = (bf16[256,256]{1,0:T(8,128)(2,1)S(1)}, bf16[256,256]{1,0:T(8,128)(2,1)}, u32[]{:S(2)}) copy-start(bf16[256,256]{1,0:T(8,128)(2,1)} %constant.19.clone.back_zero) | copy-start | bytes 393220
  14.7 84.2 %copy-start.9 = (bf16[256,256]{1,0:T(8,128)(2,1)S(1)}, bf16[256,256]{1,0:T(8,128)(2,1)}, u32[]{:S(2)}) copy-start(bf16[256,256]{1,0:T(8,128)(2,1)} %constant.20.clone.back_two) | copy-start | bytes 393220
  14.7 84.2 %copy-start.10 = (f32[2,384]{1,0:T(2,128)S(1)}, f32[2,384]{1,0:T(2,128)}, u32[]{:S(2)}) copy-start(f32[2,384]{1,0:T(2,128)} %weight.2) | copy-start | bytes 9220
  110.7 77.9 %copy-start = (bf16[76,90,128]{2,0,1:T(8,128)(2,1)S(1)}, bf16[76,90,128]{2,0,1:T(8,128)(2,1)}, u32[]{:S(2)}) copy-start(bf16[76,90,128]{2,0,1:T(8,128)(2,1)} %param.19) | copy-start | bytes 5253124
  110.7 77.9 %copy-start.11 = (bf16[4,128]{1,0:T(4,128)(2,1)S(1)}, bf16[4,128]{1,0:T(4,128)(2,1)}, u32[]{:S(2)}) copy-start(bf16[4,128]{1,0:T(4,128)(2,1)} %weight.3) | copy-start | bytes 3076
  192.3 11.7 %collective-permute-start.4 = (bf16[448,128]{1,0:T(8,128)(2,1)S(1)}, bf16[448,128]{1,0:T(8,128)(2,1)S(1)}, u32[]{:S(2)}, u32[]{:S(2)}) collective-permute-start(bf16[448,128]{1,0:T(8,128)(2,1)S(1)} %get-tuple-element.37), channel_id=1, source_target_pairs={{0,1},{1,2},{2,3},{3,4},{4,5},{5,6},{6,7},{7,0},{8,9},{9,10},{10,1... | collective-permute-start | bytes 344072 | tf_op jit(solution)/shard_map/ppermute | solution.py:732
  193.6 10.3 %collective-permute-start.6 = (bf16[448,128]{1,0:T(8,128)(2,1)S(1)}, bf16[448,128]{1,0:T(8,128)(2,1)S(1)}, u32[]{:S(2)}, u32[]{:S(2)}) collective-permute-start(bf16[448,128]{1,0:T(8,128)(2,1)S(1)} %get-tuple-element.38), channel_id=1, source_target_pairs={{1,0},{2,1},{3,2},{4,3},{5,4},{6,5},{7,6},{0,7},{9,8},{10,9},{11,1... | collective-permute-start | bytes 344072 | tf_op jit(solution)/shard_map/ppermute | solution.py:734
  193.6 10.3 %copy-start.5 = (s32[90,128]{1,0:T(8,128)S(1)}, s32[90,128]{1,0:T(8,128)}, u32[]{:S(2)}) copy-start(s32[90,128]{1,0:T(8,128)} %mask.3) | copy-start | bytes 138244
  193.6 6.3 %collective-permute-start.3 = (bf16[368,128]{1,0:T(8,128)(2,1)S(1)}, bf16[368,128]{1,0:T(8,128)(2,1)S(1)}, u32[]{:S(2)}, u32[]{:S(2)}) collective-permute-start(bf16[368,128]{1,0:T(8,128)(2,1)S(1)} %get-tuple-element.32.own), channel_id=1, source_target_pairs={{0,64},{64,0},{1,65},{65,1},{2,66},{66,2},{3,67},{67,3},{4,68},{68... | collective-permute-start | bytes 282632 | tf_op jit(solution)/shard_map/ppermute | solution.py:731
  194.9 9.1 %collective-permute-start.5 = (bf16[368,128]{1,0:T(8,128)(2,1)S(1)}, bf16[368,128]{1,0:T(8,128)(2,1)S(1)}, u32[]{:S(2)}, u32[]{:S(2)}) collective-permute-start(bf16[368,128]{1,0:T(8,128)(2,1)S(1)} %get-tuple-element.32.own), channel_id=1, source_target_pairs={{0,65},{1,66},{2,67},{3,68},{4,69},{5,70},{6,71},{7,64},{64,1},{65... | collective-permute-start | bytes 282632 | tf_op jit(solution)/shard_map/ppermute | solution.py:733
  196.8 7.1 %collective-permute-start.7 = (bf16[368,128]{1,0:T(8,128)(2,1)S(1)}, bf16[368,128]{1,0:T(8,128)(2,1)S(1)}, u32[]{:S(2)}, u32[]{:S(2)}) collective-permute-start(bf16[368,128]{1,0:T(8,128)(2,1)S(1)} %get-tuple-element.32.own), channel_id=1, source_target_pairs={{0,71},{1,64},{2,65},{3,66},{4,67},{5,68},{6,69},{7,70},{64,7},{65... | collective-permute-start | bytes 282632 | tf_op jit(solution)/shard_map/ppermute | solution.py:735

commit v3 on v2

--- a/solution.py
+++ b/solution.py
@@ -73,24 +73,24 @@
     return np.stack(made)
 
 
+def even(axis):
+    return lax.rem(lax.axis_index(axis), 2) == 0
+
+
 def pack_kernel(
     atmos,
     cotangent,
     ocean,
     mask,
     coupling,
-    conv,
-    head,
     out,
-    weights,
-    below,
-    above,
+    border_one,
+    border_two,
     in_a,
     in_c,
     warm,
     sea_cells,
     gains,
-    decoder,
     held_a,
     held_c,
     last,
@@ -108,11 +108,10 @@
         pltpu.make_async_copy(mask, sea_cells, sems.at[2, 1]),
         pltpu.make_async_copy(coupling, gains, sems.at[2, 2]),
     ]
+    facing = jnp.where(even("lat"), ROWS - 1, 0)
     others = [
-        pltpu.make_async_copy(conv, weights.at[pl.ds(0, 720)], sems.at[2, 3]),
-        pltpu.make_async_copy(head, decoder, sems.at[2, 4]),
-        pltpu.make_async_copy(ocean.at[pl.ds(ROWS - 1, 1)], below, sems.at[2, 5]),
-        pltpu.make_async_copy(ocean.at[pl.ds(0, 1)], above, sems.at[3, 0]),
+        pltpu.make_async_copy(ocean.at[pl.ds(facing, 1)], border_one, sems.at[2, 5]),
+        pltpu.make_async_copy(ocean.at[pl.ds(ROWS - 1 - facing, 1)], border_two, sems.at[3, 0]),
     ]
     for copy in surface:
         copy.start()
@@ -158,9 +157,6 @@
 
     for copy in others:
         copy.wait()
-    weights[720:800, :] = jnp.concatenate(
-        [decoder[...].astype(F32), jnp.zeros((4, 128), F32)], axis=0
-    ).astype(BF16)
 
 
 def vmem():
@@ -175,15 +171,14 @@
     return pl.BlockSpec(memory_space=pltpu.HBM)
 
 
-def pack(atmos, cotangent, ocean, sea_mask, coupling, conv, head):
-    given = (atmos, cotangent, ocean, sea_mask, coupling[None, :], conv, head)
+def pack(atmos, cotangent, ocean, sea_mask, coupling):
+    given = (atmos, cotangent, ocean, sea_mask, coupling[None, :])
     return pl.pallas_call(
         pack_kernel,
-        in_specs=[in_hbm()] * 7,
-        out_specs=[vmem()] * 4,
+        in_specs=[in_hbm()] * 5,
+        out_specs=[vmem()] * 3,
         out_shape=[
             pltpu.VMEM((OWNERS, SENT, COLS), BF16),
-            pltpu.VMEM((800, 128), BF16),
             pltpu.VMEM((1, 76, COLS), BF16),
             pltpu.VMEM((1, 76, COLS), BF16),
         ],
@@ -193,7 +188,6 @@
             pltpu.VMEM((ROWS, 16, COLS), BF16),
             pltpu.VMEM((ROWS, COLS), jnp.int32),
             pltpu.VMEM((1, CH), F32),
-            pltpu.VMEM((76, 128), BF16),
             pltpu.VMEM((16 * PITCH, COLS), F32),
             pltpu.VMEM((16 * PITCH, COLS), F32),
             pltpu.VMEM((OWNERS, 8, COLS), F32),
@@ -427,16 +421,23 @@
     return finish
 
 
+def outside_rows(got_one, got_two):
+    one, two = got_one[0], got_two[0]
+    return jnp.where(even("lat"), two, one), jnp.where(even("lat"), one, two)
+
+
 def unpack_flux_kernel(
     sent_back,
     weight,
     ocean,
-    top,
-    bottom,
+    got_one,
+    got_two,
+    head,
     out,
     flux,
-    to_east,
-    to_west,
+    to_group,
+    to_near,
+    to_far,
     held,
     staged,
     outside,
@@ -467,18 +468,21 @@
         )
 
     blank = jnp.zeros((76, COLS), BF16)
-    edges = gather(jnp.int32(0), top[0], (blank, blank))
-    edges = gather(jnp.int32(91), bottom[0], edges)
+    top, bottom = outside_rows(got_one, got_two)
+    edges = gather(jnp.int32(0), top, (blank, blank))
+    edges = gather(jnp.int32(91), bottom, edges)
     edges = lax.fori_loop(
         0, ROWS, lambda row, kept: gather(row + 1, ocean[row], kept), edges, unroll=18
     )
 
     sums = found[...].astype(BF16)
     flux[...] = sums
-    for side, message in enumerate((to_east, to_west)):
+    near_edge = jnp.where(even("lon"), edges[0], edges[1])
+    far_edge = jnp.where(even("lon"), edges[1], edges[0])
+    for message, rows in ((to_near, near_edge), (to_far, far_edge), (to_group, head[...])):
         message[0:368, :] = sums
         message[368:448, :] = jnp.concatenate(
-            [edges[side].astype(F32), jnp.zeros((4, COLS), F32)], axis=0
+            [rows.astype(F32), jnp.zeros((4, COLS), F32)], axis=0
         ).astype(BF16)
     finish()
 
@@ -488,12 +492,11 @@
     weights,
     weights_other,
     ocean,
-    top,
-    bottom,
+    got_one,
+    got_two,
     out,
     taps,
     conv,
-    head,
     held,
     staged,
     sems,
@@ -502,9 +505,8 @@
 
     for half, given in enumerate((weights, weights_other)):
         rows = slice(128 * half, 128 * half + 128)
-        wide = jnp.concatenate([given[0:720, :].astype(F32), jnp.zeros((48, 128), F32)], axis=0)
+        wide = jnp.concatenate([given[...].astype(F32), jnp.zeros((48, 128), F32)], axis=0)
         conv[rows, :] = wide.T.astype(BF16)
-        head[:, rows] = given[720:800, :]
 
     def build(row, cells):
         wide = jnp.concatenate([cells, jnp.zeros((4, COLS), BF16)], axis=0)
@@ -513,8 +515,9 @@
         taps[pl.ds(base + 80, 80), :] = wide
         taps[pl.ds(base + 160, 80), :] = pltpu.roll(wide, COLS - 1, 1)
 
-    build(0, top[0])
-    build(91, bottom[0])
+    top, bottom = outside_rows(got_one, got_two)
+    build(0, top)
+    build(91, bottom)
     taps[92 * 240 :, :] = jnp.zeros((48, COLS), BF16)
 
     @pl.loop(0, ROWS, unroll=18)
@@ -528,14 +531,15 @@
     return [pltpu.VMEM((16 * PITCH, COLS), F32), pltpu.VMEM((ROWS, CH, COLS), BF16)]
 
 
-def unpack_flux(sent_back, weight, ocean, top, bottom):
+def unpack_flux(sent_back, weight, ocean, top, bottom, head):
     return pl.pallas_call(
         unpack_flux_kernel,
-        in_specs=[vmem()] * 5,
-        out_specs=[in_hbm(), vmem(), vmem(), vmem()],
+        in_specs=[vmem()] * 6,
+        out_specs=[in_hbm(), vmem(), vmem(), vmem(), vmem()],
         out_shape=[
             jax.ShapeDtypeStruct((ROWS, CH, COLS), BF16),
             jax.ShapeDtypeStruct((368, COLS), BF16),
+            jax.ShapeDtypeStruct((448, COLS), BF16),
             jax.ShapeDtypeStruct((448, COLS), BF16),
             jax.ShapeDtypeStruct((448, COLS), BF16),
         ],
@@ -547,19 +551,18 @@
         ],
         compiler_params=pltpu.CompilerParams(vmem_limit_bytes=12 * MIB),
         name="unpack_flux",
-    )(near(sent_back), weight, near(ocean), top, bottom)
+    )(near(sent_back), weight, near(ocean), top, bottom, head)
 
 
 def unpack_taps(sent_back, weights, weights_other, ocean, top, bottom):
     return pl.pallas_call(
         unpack_taps_kernel,
         in_specs=[vmem()] * 6,
-        out_specs=[in_hbm(), vmem(), vmem(), vmem()],
+        out_specs=[in_hbm(), vmem(), vmem()],
         out_shape=[
             jax.ShapeDtypeStruct((ROWS, CH, COLS), BF16),
             pltpu.VMEM((92 * 240 + 48, COLS), BF16),
             pltpu.VMEM((256, 768), BF16),
-            pltpu.VMEM((80, 256), BF16),
         ],
         scratch_shapes=unpack_scratch() + [pltpu.SemaphoreType.DMA((6,))],
         compiler_params=pltpu.CompilerParams(vmem_limit_bytes=12 * MIB),
@@ -571,42 +574,47 @@
 def ocean_kernel(
     own,
     other,
-    left,
-    left_other,
-    right,
-    right_other,
+    near_one,
+    near_other,
+    far_one,
+    far_other,
     unfinished,
     conv,
-    head,
     ocean,
     mask,
     out,
     taps,
+    head,
     fluxes,
     hidden,
     staged,
     sems,
 ):
     def whole(one, two):
-        total = one[0:368, :].astype(F32) + two[...].astype(F32)
+        total = one[0:368, :].astype(F32) + two[0:368, :].astype(F32)
         return total.astype(BF16).astype(F32)
 
     column = lax.broadcasted_iota(jnp.int32, (368, COLS), 1)
+    def sides(one, two):
+        return jnp.where(even("lon"), two, one), jnp.where(even("lon"), one, two)
+
     middle = whole(own, other)
-    west = pltpu.roll(whole(left, left_other), 1, 1)
-    east = pltpu.roll(whole(right, right_other), COLS - 1, 1)
+    west, east = sides(whole(near_one, near_other), whole(far_one, far_other))
+    west = pltpu.roll(west, 1, 1)
+    east = pltpu.roll(east, COLS - 1, 1)
     fluxes[0] = jnp.where(column == 0, west, pltpu.roll(middle, 1, 1))
     fluxes[1] = middle
     fluxes[2] = jnp.where(column == COLS - 1, east, pltpu.roll(middle, COLS - 1, 1))
 
+    head[:, 0:128] = own[368:448, :]
+    head[:, 128:256] = other[368:448, :]
+
     lane = lax.broadcasted_iota(jnp.int32, (80, COLS), 1)
-    first_edge = left[368:448, :]
-    final_edge = right[368:448, :]
+    first_edge, final_edge = sides(near_one[368:448, :], far_one[368:448, :])
 
     taps[92 * 240 :, :] = jnp.zeros((48, COLS), BF16)
 
-    @pl.loop(0, ROWS + 2, unroll=23)
-    def _(row):
+    def complete(row):
         base = pl.multiple_of(240 * row, 16)
         first = pltpu.roll(first_edge, lax.rem(COLS - row, COLS), 1)
         final = pltpu.roll(final_edge, COLS - 1 - row, 1)
@@ -628,7 +636,7 @@
     def window(row):
         return taps[pl.ds(pl.multiple_of(240 * row, 16), 768), :]
 
-    def convolve(g):
+    def convolve(g, more):
         for pair in range(5):
             first = 10 * g + 2 * pair
             around = jnp.concatenate([window(first), window(first + 1)], axis=1)
@@ -638,6 +646,9 @@
             hidden[lax.rem(g, 2), :, 256 * pair : 256 * pair + 256] = (half + half * bent).astype(
                 BF16
             )
+            if more:
+                for k in range(2):
+                    complete(first + 12 + k)
 
     def decode(g):
         delta = jnp.dot(head[...], hidden[lax.rem(g, 2)], preferred_element_type=F32)
@@ -649,26 +660,31 @@
             ).astype(BF16)
         send(g).start()
 
-    convolve(jnp.int32(0))
-
-    @pl.loop(1, 9)
+    for row in range(12):
+        complete(jnp.int32(row))
+    convolve(jnp.int32(0), True)
+
+    @pl.loop(1, 8)
     def _(g):
-        convolve(g)
+        convolve(g, True)
         decode(g - 1)
 
+    convolve(jnp.int32(8), False)
+    decode(jnp.int32(7))
     decode(jnp.int32(8))
     for g in range(9):
         send(g).wait()
 
 
-def ocean_step(fluxes, taps, conv, head, ocean, sea_mask):
+def ocean_step(fluxes, taps, conv, ocean, sea_mask):
     return pl.pallas_call(
         ocean_kernel,
-        in_specs=[vmem()] * 11,
+        in_specs=[vmem()] * 10,
         out_specs=in_hbm(),
         out_shape=jax.ShapeDtypeStruct((ROWS, 76, COLS), BF16),
         scratch_shapes=[
             pltpu.VMEM((92 * 240 + 48, COLS), BF16),
+            pltpu.VMEM((80, 256), BF16),
             pltpu.VMEM((3, 368, COLS), F32),
             pltpu.VMEM((2, 256, 1280), BF16),
             pltpu.VMEM((ROWS, 76, COLS), BF16),
@@ -676,7 +692,7 @@
         ],
         compiler_params=pltpu.CompilerParams(vmem_limit_bytes=14 * MIB),
         name="ocean",
-    )(*fluxes, near(taps), near(conv), near(head), near(ocean), sea_mask)
+    )(*fluxes, near(taps), near(conv), near(ocean), sea_mask)
 
 
 def after(value, *others):
@@ -697,47 +713,46 @@
     atmos = atmos.transpose(1, 0, 2)
     cotangent = cotangent.transpose(1, 0, 2)
     ocean = ocean.transpose(1, 0, 2)
-    ring = range(8)
-    east = [(k, (k + 1) % 8) for k in ring]
-    west = [((k + 1) % 8, k) for k in ring]
+    near_pairs = [(k, k ^ 1) for k in range(8)]
+    far_pairs = [(k, (k + 1 - 2 * (k % 2 == 0)) % 8) for k in range(8)]
     swap = [(0, 1), (1, 0)]
     lon_table, lat_table = make_tables(NLAT, NLON, KMODES, LDEG)
 
-    sent, weights, below, above = pack(
-        atmos,
-        cotangent,
-        ocean,
-        sea_mask,
-        coupling,
-        conv_weight.reshape(720, 128),
-        head_weight.T,
-    )
-    weights_other = lax.ppermute(weights, "group", swap)
-    top = lax.ppermute(below, "lat", [(k, k + 1) for k in range(7)])
-    bottom = lax.ppermute(above, "lat", [(k + 1, k) for k in range(7)])
-    sent, weights_other, top, bottom = lax.optimization_barrier(
-        (sent, weights_other, top, bottom)
-    )
+    barrier = lax.optimization_barrier
+    sent, border_one, border_two = pack(atmos, cotangent, ocean, sea_mask, coupling)
     got = lax.all_to_all(sent, ("lat", "lon"), split_axis=0, concat_axis=0, tiled=True)
+
+    conv = conv_weight.reshape(720, 128)
+    got, conv, border_one, border_two = barrier((got, conv, border_one, border_two))
+    conv_other = lax.ppermute(conv, "group", swap)
+    got_one = lax.ppermute(border_one, "lat", near_pairs)
+    got_two = lax.ppermute(border_two, "lat", [pair for pair in far_pairs if set(pair) != {0, 7}])
     sent_back, grad_spectral = spectral(
         got, arrange_lon(lon_table), arrange_lat(lat_table), spectral_weight
     )
+    sent_back, conv_other, got_one, got_two = barrier(
+        (sent_back, conv_other, got_one, got_two)
+    )
     returned = lax.all_to_all(sent_back, ("lat", "lon"), split_axis=0, concat_axis=0, tiled=True)
-    atmos_next, flux, to_east, to_west = unpack_flux(returned, flux_weight, ocean, top, bottom)
-    across = [(8 * g + k, 8 * (1 - g) + (k + 1) % 8) for g in range(2) for k in ring]
-    counter = [(8 * g + k, 8 * (1 - g) + (k - 1) % 8) for g in range(2) for k in ring]
+    atmos_next, flux, to_group, to_near, to_far = unpack_flux(
+        returned, flux_weight, ocean, got_one, got_two, head_weight.T
+    )
+
+    def crossed(pairs):
+        return [(8 * g + k, 8 * (1 - g) + to) for g in range(2) for k, to in pairs]
+
     fluxes = [
-        flux,
-        lax.ppermute(flux, "group", swap),
-        lax.ppermute(to_east, "lon", east),
-        lax.ppermute(flux, ("group", "lon"), across),
-        lax.ppermute(to_west, "lon", west),
-        lax.ppermute(flux, ("group", "lon"), counter),
+        to_group,
+        lax.ppermute(to_group, "group", swap),
+        lax.ppermute(to_near, "lon", near_pairs),
+        lax.ppermute(flux, ("group", "lon"), crossed(near_pairs)),
+        lax.ppermute(to_far, "lon", far_pairs),
+        lax.ppermute(flux, ("group", "lon"), crossed(far_pairs)),
     ]
-    grad_atmos, taps, conv, head = unpack_taps(
-        after(returned, flux), weights, weights_other, ocean, top, bottom
-    )
-    ocean_next = ocean_step(fluxes, taps, conv, head, ocean, sea_mask)
+    grad_atmos, taps, conv = unpack_taps(
+        after(returned, flux), conv, conv_other, ocean, got_one, got_two
+    )
+    ocean_next = ocean_step(fluxes, taps, conv, ocean, sea_mask)
     return (
         atmos_next.transpose(1, 0, 2),
         grad_atmos.transpose(1, 0, 2),

time: 216 us -> 208 us (0.963)
  starting transfers between devices: 12.4 us -> 7.17 us
  waiting for transfers between devices: 7.42 us -> 3.13 us
    ppermute x8, starting transfers between devices: 12.4 us -> 7.17 us  [the longest x1 1.89 us: local(): lax.ppermute(to_far, 'lon', far_pairs)]
    ppermute x8, waiting for transfers between devices: 7.42 us -> 3.13 us  [the longest x1 1.85 us: local(): lax.ppermute(flux, ('group', 'lon'), crossed(far_pairs))]
    all_to_all x1, blocking collectives: 77.9 us -> 81.7 us  [local(): lax.all_to_all(sent_back, ('lat', 'lon'), split_axis=0, concat_axis=0, ti...]
  transfers between devices with their start and end apart: 8 -> 8, of which waited for: 2 -> 2; matrix products, arithmetic and copies ran while one was open for 0% -> 0% of each run, Pallas kernels for 1% -> 7%
where the time goes in v3:
time: 208 us
  blocking collectives  164 us (79%)
  Pallas kernels  31.7 us (15%)
  starting transfers between devices  7.17 us (3%)
  waiting for transfers between devices  3.13 us (2%)
    all_to_all x1, blocking collectives, local(): lax.all_to_all(sent, ('lat', 'lon'), split_axis=0, concat_axis=0, tiled=T...  82.8 us
    all_to_all x1, blocking collectives, local(): lax.all_to_all(sent_back, ('lat', 'lon'), split_axis=0, concat_axis=0, ti...  81.7 us
    pallas_call x1, Pallas kernels, spectral(): pl.pallas_call(spectral_kernel, in_specs=[vmem()] * 10, out_specs=[vmem()...  11.8 us
    pallas_call x1, Pallas kernels, ocean_step(): pl.pallas_call(ocean_kernel, in_specs=[vmem()] * 10, out_specs=in_hbm(),...  10.5 us
  transfers between devices with their start and end apart: 8, of which 2 were waited for; matrix products, arithmetic and copies ran while one was open for 0% of the time, Pallas kernels for 7%

profile of v3, /device:TPU:1, one launch (start us, length us, event | category | flops | bytes accessed | tf_op | source)
XLA Modules:
  0.0 207.6 jit_solution(10278382009231787493)
XLA Ops:
  0.6 3.5 %pack.1 = (bf16[64,360,128]{2,1,0:T(8,128)(2,1)S(1)}, bf16[1,76,128]{2,1,0:T(8,128)(2,1)S(1)}, bf16[1,76,128]{2,1,0:T(8,128)(2,1)S(1)}) custom-call(bf16[90,128,128]{2,1,0:T(8,128)(2,1)} %bitcast.16, bf16[90,128,128]{2,1,0:T(8,128)(2,1)} %bitcast.17, bf16[90,76,128]{2,1,0:T(8,128)(2,1)} %bitcast.9, s32[90,128]{1,0:T(8,128)} %mask.3, f32[1,128]{1,0:T(1,128)} %bitcast.19), custom_call_target="tpu_custom_call" | custom-call | tf_op jit(solution)/shard_map/pack/pallas_call | solution.py:176
  4.2 0.0 copy-start.6
  4.2 0.0 copy-start.1
  4.2 0.0 copy-start.2
  4.2 0.0 copy-start.3
  4.2 0.0 copy-start.4
  4.2 0.0 copy-start.7
  4.2 0.0 copy-start.8
  4.3 0.0 copy-start.9
  4.3 0.0 copy-start.10
  4.3 0.0 copy-start.12
  4.3 82.8 %all_to_all.10.got = bf16[64,360,128]{2,1,0:T(8,128)(2,1)S(1)} all-to-all(bf16[64,360,128]{2,1,0:T(8,128)(2,1)S(1)} %get-tuple-element.26), channel_id=1, replica_groups=mesh['group'=2,'lat'=8,'lon'=8] {'lat','lon'}, dimensions={0} | all-to-all | bytes 11796480 | tf_op jit(solution)/shard_map/all_to_all | solution.py:723
  87.1 0.0 copy-done.6
  87.1 0.4 collective-permute-start
  87.5 1.1 collective-permute-start.1
  88.5 0.7 collective-permute-start.2
  89.2 0.0 copy-done.1
  89.2 0.0 copy-done.2
  89.2 0.0 copy-done.3
  89.2 0.0 copy-done.4
  89.2 0.0 copy-done.7
  89.2 0.0 copy-done.8
  89.3 0.0 copy-done.9
  89.3 0.0 copy-done.10
  89.3 0.0 copy-done.12
  89.3 11.8 %spectral.1 = (bf16[64,368,128]{2,1,0:T(8,128)(2,1)S(1)}, f32[2,384]{1,0:T(2,128)}) custom-call(bf16[64,360,128]{2,1,0:T(8,128)(2,1)S(1)} %all_to_all.10.got, bf16[256,256]{1,0:T(8,128)(2,1)S(1)} %copy-done.7, bf16[256,256]{1,0:T(8,128)(2,1)S(1)} %copy-done.8, bf16[512,384]{1,0:T(8,128)(2,1)S(1)} %copy-done.3, bf16[256,256]{1,0:T(8,128)(2,1)S(1)} %copy-done.9, ...), custom_call_target="tpu_custom_call" | custom-call | tf_op jit(solution)/shard_map/spectral/pallas_call | solution.py:358
  101.1 0.0 collective-permute-done.1.got_one
  101.1 0.0 collective-permute-done.2.got_two
  101.1 0.0 collective-permute-done.weights_other
  101.1 0.0 copy-start
  101.1 0.0 copy-start.11
  101.1 0.0 copy-start.13
  101.1 81.7 %all_to_all.11.sent_back = bf16[64,368,128]{2,1,0:T(8,128)(2,1)S(1)} all-to-all(bf16[64,368,128]{2,1,0:T(8,128)(2,1)S(1)} %get-tuple-element.34), channel_id=1, replica_groups=mesh['group'=2,'lat'=8,'lon'=8] {'lat','lon'}, dimensions={0} | all-to-all | bytes 12058624 | tf_op jit(solution)/shard_map/all_to_all | solution.py:736
  182.8 0.0 copy-done
  182.8 0.0 copy-done.11
  182.8 3.6 %unpack_flux.1 = (bf16[90,128,128]{2,1,0:T(8,128)(2,1)}, bf16[368,128]{1,0:T(8,128)(2,1)S(1)}, bf16[448,128]{1,0:T(8,128)(2,1)S(1)}, bf16[448,128]{1,0:T(8,128)(2,1)S(1)}, bf16[448,128]{1,0:T(8,128)(2,1)S(1)}) custom-call(bf16[64,368,128]{2,1,0:T(8,128)(2,1)S(1)} %all_to_all.11.sent_back, bf16[4,128]{1,0:T(4,128)(2,1)S(1)} %copy-done.13, ...), custom_call_target="tpu_custom_call" | custom-call | tf_op jit(solution)/shard_map/unpack_flux/pallas_call | solution.py:535
  186.5 0.3 collective-permute-start.3
  186.8 1.1 collective-permute-start.4
  187.9 1.9 collective-permute-start.6
  189.8 1.8 collective-permute-start.5
  191.6 0.0 collective-permute-start.7
  191.6 2.3 %unpack_taps.1 = (bf16[90,128,128]{2,1,0:T(8,128)(2,1)}, bf16[22128,128]{1,0:T(8,128)(2,1)S(1)}, bf16[256,768]{1,0:T(8,128)(2,1)S(1)}) custom-call(bf16[64,368,128]{2,1,0:T(8,128)(2,1)S(1)} %all_to_all.11.sent_back, bf16[720,128]{1,0:T(8,128)(2,1)S(1)} %bitcast.14, bf16[720,128]{1,0:T(8,128)(2,1)S(1)} %collective-permute-done.weights_other, ...), custom_call_target="tpu_custom_call" | custom-call | bytes 12000000 | tf_op jit(solution)/shard_map/unpack_taps/pallas_call | solution.py:558
  193.8 1.3 collective-permute-done.5.near_other
  195.1 1.8 collective-permute-done.7.far_other
  196.9 0.0 collective-permute-done.3.other
  196.9 0.0 collective-permute-done.4.near_one
  196.9 0.0 collective-permute-done.6.far_one
  197.0 10.5 %ocean.1 = bf16[90,76,128]{2,1,0:T(8,128)(2,1)} custom-call(bf16[448,128]{1,0:T(8,128)(2,1)S(1)} %get-tuple-element.43.own, bf16[448,128]{1,0:T(8,128)(2,1)S(1)} %collective-permute-done.3.other, bf16[448,128]{1,0:T(8,128)(2,1)S(1)} %collective-permute-done.4.near_one, bf16[368,128]{1,0:T(8,128)(2,1)S(1)} %collective-permute-done.5.near_other, ...), custom_call_target="tpu_custom_call" | custom-call | tf_op jit(solution)/shard_map/ocean/pallas_call | solution.py:680
  (3 shorter events, 0.0 us)
Async XLA Ops:
  4.2 82.9 %copy-start.6 = (bf16[3,3,80,128]{3,2,1,0:T(8,128)(2,1)S(1)}, bf16[3,3,80,128]{3,2,1,0:T(8,128)(2,1)}, u32[]{:S(2)}) copy-start(bf16[3,3,80,128]{3,2,1,0:T(8,128)(2,1)} %param.24) | copy-start | bytes 552964
  4.2 85.0 %copy-start.1 = (bf16[4,384,768]{2,1,0:T(8,128)(2,1)S(1)}, bf16[4,384,768]{2,1,0:T(8,128)(2,1)}, u32[]{:S(2)}) copy-start(bf16[4,384,768]{2,1,0:T(8,128)(2,1)} %constant.22.clone.lat) | copy-start | bytes 7077892
  4.2 85.0 %copy-start.2 = (bf16[4,768,384]{2,1,0:T(8,128)(2,1)S(1)}, bf16[4,768,384]{2,1,0:T(8,128)(2,1)}, u32[]{:S(2)}) copy-start(bf16[4,768,384]{2,1,0:T(8,128)(2,1)} %constant.23.clone.lat_back) | copy-start | bytes 7077892
  4.2 85.0 %copy-start.3 = (bf16[512,384]{1,0:T(8,128)(2,1)S(1)}, bf16[512,384]{1,0:T(8,128)(2,1)}, u32[]{:S(2)}) copy-start(bf16[512,384]{1,0:T(8,128)(2,1)} %constant.18.clone.lon_odd) | copy-start | bytes 1179652
  4.2 85.0 %copy-start.4 = (bf16[384,512]{1,0:T(8,128)(2,1)S(1)}, bf16[384,512]{1,0:T(8,128)(2,1)}, u32[]{:S(2)}) copy-start(bf16[384,512]{1,0:T(8,128)(2,1)} %constant.21.clone.back_odd) | copy-start | bytes 1179652
  4.2 85.0 %copy-start.7 = (bf16[256,256]{1,0:T(8,128)(2,1)S(1)}, bf16[256,256]{1,0:T(8,128)(2,1)}, u32[]{:S(2)}) copy-start(bf16[256,256]{1,0:T(8,128)(2,1)} %constant.16.clone.lon_zero) | copy-start | bytes 393220
  4.2 85.0 %copy-start.8 = (bf16[256,256]{1,0:T(8,128)(2,1)S(1)}, bf16[256,256]{1,0:T(8,128)(2,1)}, u32[]{:S(2)}) copy-start(bf16[256,256]{1,0:T(8,128)(2,1)} %constant.17.clone.lon_two) | copy-start | bytes 393220
  4.3 85.0 %copy-start.9 = (bf16[256,256]{1,0:T(8,128)(2,1)S(1)}, bf16[256,256]{1,0:T(8,128)(2,1)}, u32[]{:S(2)}) copy-start(bf16[256,256]{1,0:T(8,128)(2,1)} %constant.19.clone.back_zero) | copy-start | bytes 393220
  4.3 85.0 %copy-start.10 = (bf16[256,256]{1,0:T(8,128)(2,1)S(1)}, bf16[256,256]{1,0:T(8,128)(2,1)}, u32[]{:S(2)}) copy-start(bf16[256,256]{1,0:T(8,128)(2,1)} %constant.20.clone.back_two) | copy-start | bytes 393220
  4.3 85.0 %copy-start.12 = (f32[2,384]{1,0:T(2,128)S(1)}, f32[2,384]{1,0:T(2,128)}, u32[]{:S(2)}) copy-start(f32[2,384]{1,0:T(2,128)} %weight.2) | copy-start | bytes 9220
  87.1 14.0 %collective-permute-start = (bf16[720,128]{1,0:T(8,128)(2,1)S(1)}, bf16[720,128]{1,0:T(8,128)(2,1)S(1)}, u32[]{:S(2)}, u32[]{:S(2)}) collective-permute-start(bf16[720,128]{1,0:T(8,128)(2,1)S(1)} %bitcast.13), channel_id=1, source_target_pairs={{0,64},{64,0},{1,65},{65,1},{2,66},{66,2},{3,67},{67,3},{4,68},{68... | collective-permute-start | bytes 552968 | tf_op jit(solution)/shard_map/ppermute | solution.py:727
  87.5 13.6 %collective-permute-start.1 = (bf16[1,76,128]{2,1,0:T(8,128)(2,1)S(1)}, bf16[1,76,128]{2,1,0:T(8,128)(2,1)S(1)}, u32[]{:S(2)}, u32[]{:S(2)}) collective-permute-start(bf16[1,76,128]{2,1,0:T(8,128)(2,1)S(1)} %get-tuple-element.32), channel_id=1, source_target_pairs={{0,8},{8,0},{16,24},{24,16},{32,40},{40,32},{48,56},{56,48},{1,9},... | collective-permute-start | bytes 58376 | tf_op jit(solution)/shard_map/ppermute | solution.py:728
  88.5 12.5 %collective-permute-start.2 = (bf16[1,76,128]{2,1,0:T(8,128)(2,1)S(1)}, bf16[1,76,128]{2,1,0:T(8,128)(2,1)S(1)}, u32[]{:S(2)}, u32[]{:S(2)}) collective-permute-start(bf16[1,76,128]{2,1,0:T(8,128)(2,1)S(1)} %get-tuple-element.33), channel_id=1, source_target_pairs={{8,16},{16,8},{24,32},{32,24},{40,48},{48,40},{9,17},{17,9},{25,33... | collective-permute-start | bytes 58376 | tf_op jit(solution)/shard_map/ppermute | solution.py:729
  101.1 81.7 %copy-start = (bf16[76,90,128]{2,0,1:T(8,128)(2,1)S(1)}, bf16[76,90,128]{2,0,1:T(8,128)(2,1)}, u32[]{:S(2)}) copy-start(bf16[76,90,128]{2,0,1:T(8,128)(2,1)} %param.19) | copy-start | bytes 5253124
  101.1 81.7 %copy-start.11 = (bf16[128,76]{0,1:T(8,128)(2,1)S(1)}, bf16[128,76]{0,1:T(8,128)(2,1)}, u32[]{:S(2)}) copy-start(bf16[128,76]{0,1:T(8,128)(2,1)} %param.25) | copy-start | bytes 58372
  101.1 81.7 %copy-start.13 = (bf16[4,128]{1,0:T(4,128)(2,1)S(1)}, bf16[4,128]{1,0:T(4,128)(2,1)}, u32[]{:S(2)}) copy-start(bf16[4,128]{1,0:T(4,128)(2,1)} %weight.3) | copy-start | bytes 3076
  186.5 10.5 %collective-permute-start.3 = (bf16[448,128]{1,0:T(8,128)(2,1)S(1)}, bf16[448,128]{1,0:T(8,128)(2,1)S(1)}, u32[]{:S(2)}, u32[]{:S(2)}) collective-permute-start(bf16[448,128]{1,0:T(8,128)(2,1)S(1)} %get-tuple-element.43.own), channel_id=1, source_target_pairs={{0,64},{64,0},{1,65},{65,1},{2,66},{66,2},{3,67},{67,3},{4,68},{68... | collective-permute-start | bytes 344072 | tf_op jit(solution)/shard_map/ppermute | solution.py:746
  186.8 10.1 %collective-permute-start.4 = (bf16[448,128]{1,0:T(8,128)(2,1)S(1)}, bf16[448,128]{1,0:T(8,128)(2,1)S(1)}, u32[]{:S(2)}, u32[]{:S(2)}) collective-permute-start(bf16[448,128]{1,0:T(8,128)(2,1)S(1)} %get-tuple-element.44), channel_id=1, source_target_pairs={{0,1},{1,0},{2,3},{3,2},{4,5},{5,4},{6,7},{7,6},{8,9},{9,8},{10,11... | collective-permute-start | bytes 344072 | tf_op jit(solution)/shard_map/ppermute | solution.py:747
  187.9 9.1 %collective-permute-start.6 = (bf16[448,128]{1,0:T(8,128)(2,1)S(1)}, bf16[448,128]{1,0:T(8,128)(2,1)S(1)}, u32[]{:S(2)}, u32[]{:S(2)}) collective-permute-start(bf16[448,128]{1,0:T(8,128)(2,1)S(1)} %get-tuple-element.45), channel_id=1, source_target_pairs={{0,7},{1,2},{2,1},{3,4},{4,3},{5,6},{6,5},{7,0},{8,15},{9,10},{10,... | collective-permute-start | bytes 344072 | tf_op jit(solution)/shard_map/ppermute | solution.py:749
  189.8 7.2 %copy-start.5 = (s32[90,128]{1,0:T(8,128)S(1)}, s32[90,128]{1,0:T(8,128)}, u32[]{:S(2)}) copy-start(s32[90,128]{1,0:T(8,128)} %mask.3) | copy-start | bytes 138244
  189.8 5.3 %collective-permute-start.5 = (bf16[368,128]{1,0:T(8,128)(2,1)S(1)}, bf16[368,128]{1,0:T(8,128)(2,1)S(1)}, u32[]{:S(2)}, u32[]{:S(2)}) collective-permute-start(bf16[368,128]{1,0:T(8,128)(2,1)S(1)} %get-tuple-element.38), channel_id=1, source_target_pairs={{0,65},{1,64},{2,67},{3,66},{4,69},{5,68},{6,71},{7,70},{64,1},{65... | collective-permute-start | bytes 282632 | tf_op jit(solution)/shard_map/ppermute | solution.py:748
  191.6 5.4 %collective-permute-start.7 = (bf16[368,128]{1,0:T(8,128)(2,1)S(1)}, bf16[368,128]{1,0:T(8,128)(2,1)S(1)}, u32[]{:S(2)}, u32[]{:S(2)}) collective-permute-start(bf16[368,128]{1,0:T(8,128)(2,1)S(1)} %get-tuple-element.38), channel_id=1, source_target_pairs={{0,71},{1,66},{2,65},{3,68},{4,67},{5,70},{6,69},{7,64},{64,7},{65... | collective-permute-start | bytes 282632 | tf_op jit(solution)/shard_map/ppermute | solution.py:750

commit v4 on v3

--- a/solution.py
+++ b/solution.py
@@ -224,7 +224,7 @@
     def dot(one, two):
         return jnp.dot(one, two, preferred_element_type=F32)
 
-    @pl.loop(0, 4)
+    @pl.loop(0, 4, unroll=4)
     def _(p):
         found = []
         for a in range(2):
@@ -323,7 +323,7 @@
         lanes = slice(128 * o, 128 * o + 256)
         halo[:, :, lanes] = found.reshape(8, 8, 256) + edge_in[1:9, :, lanes]
 
-    @pl.loop(0, 4)
+    @pl.loop(0, 4, unroll=4)
     def _(p):
         for first, found in inverse(back[p]):
             for half in range(2):
@@ -400,7 +400,7 @@
         span = pl.ds(16 * i, rows)
         return pltpu.make_async_copy(staged.at[span], out.at[span], sems.at[i])
 
-    @pl.loop(0, 5)
+    @pl.loop(0, 5, unroll=5)
     def _(i):
         spread(sent_back, i, field, held)
         for r in range(16):
@@ -664,7 +664,7 @@
         complete(jnp.int32(row))
     convolve(jnp.int32(0), True)
 
-    @pl.loop(1, 8)
+    @pl.loop(1, 8, unroll=7)
     def _(g):
         convolve(g, True)
         decode(g - 1)

time: 208 us -> 203 us (0.976)
  Pallas kernels: 31.7 us -> 26.9 us
    pallas_call x1, Pallas kernels: 10.5 us -> 7.84 us  [ocean_step(): pl.pallas_call(ocean_kernel, in_specs=[vmem()] * 10, out_specs=in_hbm(),...]
  transfers between devices with their start and end apart: 8 -> 8, of which waited for: 2 -> 2; matrix products, arithmetic and copies ran while one was open for 0% -> 0% of each run, Pallas kernels for 7% -> 6%
where the time goes in v4:
time: 203 us
  blocking collectives  164 us (81%)
  Pallas kernels  26.9 us (13%)
  starting transfers between devices  7.57 us (4%)
  waiting for transfers between devices  2.96 us (1%)
    all_to_all x1, blocking collectives, local(): lax.all_to_all(sent, ('lat', 'lon'), split_axis=0, concat_axis=0, tiled=T...  82.8 us
    all_to_all x1, blocking collectives, local(): lax.all_to_all(sent_back, ('lat', 'lon'), split_axis=0, concat_axis=0, ti...  81.7 us
    pallas_call x1, Pallas kernels, spectral(): pl.pallas_call(spectral_kernel, in_specs=[vmem()] * 10, out_specs=[vmem()...  10.3 us
    pallas_call x1, Pallas kernels, ocean_step(): pl.pallas_call(ocean_kernel, in_specs=[vmem()] * 10, out_specs=in_hbm(),...  7.84 us
  transfers between devices with their start and end apart: 8, of which 2 were waited for; matrix products, arithmetic and copies ran while one was open for 0% of the time, Pallas kernels for 6%

profile of v4, /device:TPU:1, one launch (start us, length us, event | category | flops | bytes accessed | tf_op | source)
XLA Modules:
  0.0 203.1 jit_solution(3761793711370454698)
XLA Ops:
  0.6 3.5 %pack.1 = (bf16[64,360,128]{2,1,0:T(8,128)(2,1)S(1)}, bf16[1,76,128]{2,1,0:T(8,128)(2,1)S(1)}, bf16[1,76,128]{2,1,0:T(8,128)(2,1)S(1)}) custom-call(bf16[90,128,128]{2,1,0:T(8,128)(2,1)} %bitcast.16, bf16[90,128,128]{2,1,0:T(8,128)(2,1)} %bitcast.17, bf16[90,76,128]{2,1,0:T(8,128)(2,1)} %bitcast.9, s32[90,128]{1,0:T(8,128)} %mask.3, f32[1,128]{1,0:T(1,128)} %bitcast.19), custom_call_target="tpu_custom_call" | custom-call | tf_op jit(solution)/shard_map/pack/pallas_call | solution.py:176
  4.2 0.0 copy-start.6
  4.2 0.0 copy-start.1
  4.2 0.0 copy-start.2
  4.2 0.0 copy-start.3
  4.2 0.0 copy-start.4
  4.2 0.0 copy-start.7
  4.2 0.0 copy-start.8
  4.3 0.0 copy-start.9
  4.3 0.0 copy-start.10
  4.3 0.0 copy-start.12
  4.3 82.8 %all_to_all.10.got = bf16[64,360,128]{2,1,0:T(8,128)(2,1)S(1)} all-to-all(bf16[64,360,128]{2,1,0:T(8,128)(2,1)S(1)} %get-tuple-element.26), channel_id=1, replica_groups=mesh['group'=2,'lat'=8,'lon'=8] {'lat','lon'}, dimensions={0} | all-to-all | bytes 11796480 | tf_op jit(solution)/shard_map/all_to_all | solution.py:723
  87.1 0.0 copy-done.6
  87.1 0.4 collective-permute-start
  87.5 1.1 collective-permute-start.1
  88.5 0.8 collective-permute-start.2
  89.4 0.0 copy-done.1
  89.4 0.0 copy-done.2
  89.4 0.0 copy-done.3
  89.4 0.0 copy-done.4
  89.4 0.0 copy-done.7
  89.4 0.0 copy-done.8
  89.4 0.0 copy-done.9
  89.5 0.0 copy-done.10
  89.5 0.0 copy-done.12
  89.5 10.3 %spectral.1 = (bf16[64,368,128]{2,1,0:T(8,128)(2,1)S(1)}, f32[2,384]{1,0:T(2,128)}) custom-call(bf16[64,360,128]{2,1,0:T(8,128)(2,1)S(1)} %all_to_all.10.got, bf16[256,256]{1,0:T(8,128)(2,1)S(1)} %copy-done.7, bf16[256,256]{1,0:T(8,128)(2,1)S(1)} %copy-done.8, bf16[512,384]{1,0:T(8,128)(2,1)S(1)} %copy-done.3, bf16[256,256]{1,0:T(8,128)(2,1)S(1)} %copy-done.9, ...), custom_call_target="tpu_custom_call" | custom-call | tf_op jit(solution)/shard_map/spectral/pallas_call | solution.py:358
  99.8 0.0 collective-permute-done.1.got_one
  99.8 0.0 collective-permute-done.2.got_two
  99.8 0.0 collective-permute-done.weights_other
  99.8 0.0 copy-start
  99.8 0.0 copy-start.11
  99.8 0.0 copy-start.13
  99.8 81.7 %all_to_all.11.sent_back = bf16[64,368,128]{2,1,0:T(8,128)(2,1)S(1)} all-to-all(bf16[64,368,128]{2,1,0:T(8,128)(2,1)S(1)} %get-tuple-element.34), channel_id=1, replica_groups=mesh['group'=2,'lat'=8,'lon'=8] {'lat','lon'}, dimensions={0} | all-to-all | bytes 12058624 | tf_op jit(solution)/shard_map/all_to_all | solution.py:736
  181.5 0.0 copy-done.11
  181.5 2.8 %unpack_flux.1 = (bf16[90,128,128]{2,1,0:T(8,128)(2,1)}, bf16[368,128]{1,0:T(8,128)(2,1)S(1)}, bf16[448,128]{1,0:T(8,128)(2,1)S(1)}, bf16[448,128]{1,0:T(8,128)(2,1)S(1)}, bf16[448,128]{1,0:T(8,128)(2,1)S(1)}) custom-call(bf16[64,368,128]{2,1,0:T(8,128)(2,1)S(1)} %all_to_all.11.sent_back, bf16[4,128]{1,0:T(4,128)(2,1)S(1)} %copy-done.13, ...), custom_call_target="tpu_custom_call" | custom-call | tf_op jit(solution)/shard_map/unpack_flux/pallas_call | solution.py:535
  184.4 0.6 collective-permute-start.3
  184.9 1.1 collective-permute-start.4
  186.0 1.9 collective-permute-start.6
  187.9 1.8 collective-permute-start.5
  189.7 0.0 collective-permute-start.7
  189.7 2.4 %unpack_taps.1 = (bf16[90,128,128]{2,1,0:T(8,128)(2,1)}, bf16[22128,128]{1,0:T(8,128)(2,1)S(1)}, bf16[256,768]{1,0:T(8,128)(2,1)S(1)}) custom-call(bf16[64,368,128]{2,1,0:T(8,128)(2,1)S(1)} %all_to_all.11.sent_back, bf16[720,128]{1,0:T(8,128)(2,1)S(1)} %bitcast.14, bf16[720,128]{1,0:T(8,128)(2,1)S(1)} %collective-permute-done.weights_other, ...), custom_call_target="tpu_custom_call" | custom-call | bytes 12000000 | tf_op jit(solution)/shard_map/unpack_taps/pallas_call | solution.py:558
  192.1 1.1 collective-permute-done.5.near_other
  193.2 1.8 collective-permute-done.7.far_other
  195.1 0.0 collective-permute-done.3.other
  195.1 0.0 collective-permute-done.4.near_one
  195.1 0.0 collective-permute-done.6.far_one
  195.1 0.0 copy-done.5
  195.1 7.8 %ocean.1 = bf16[90,76,128]{2,1,0:T(8,128)(2,1)} custom-call(bf16[448,128]{1,0:T(8,128)(2,1)S(1)} %get-tuple-element.43.own, bf16[448,128]{1,0:T(8,128)(2,1)S(1)} %collective-permute-done.3.other, bf16[448,128]{1,0:T(8,128)(2,1)S(1)} %collective-permute-done.4.near_one, bf16[368,128]{1,0:T(8,128)(2,1)S(1)} %collective-permute-done.5.near_other, ...), custom_call_target="tpu_custom_call" | custom-call | tf_op jit(solution)/shard_map/ocean/pallas_call | solution.py:680
  (3 shorter events, 0.0 us)
Async XLA Ops:
  4.2 82.9 %copy-start.6 = (bf16[3,3,80,128]{3,2,1,0:T(8,128)(2,1)S(1)}, bf16[3,3,80,128]{3,2,1,0:T(8,128)(2,1)}, u32[]{:S(2)}) copy-start(bf16[3,3,80,128]{3,2,1,0:T(8,128)(2,1)} %param.24) | copy-start | bytes 552964
  4.2 85.2 %copy-start.1 = (bf16[4,384,768]{2,1,0:T(8,128)(2,1)S(1)}, bf16[4,384,768]{2,1,0:T(8,128)(2,1)}, u32[]{:S(2)}) copy-start(bf16[4,384,768]{2,1,0:T(8,128)(2,1)} %constant.22.clone.lat) | copy-start | bytes 7077892
  4.2 85.2 %copy-start.2 = (bf16[4,768,384]{2,1,0:T(8,128)(2,1)S(1)}, bf16[4,768,384]{2,1,0:T(8,128)(2,1)}, u32[]{:S(2)}) copy-start(bf16[4,768,384]{2,1,0:T(8,128)(2,1)} %constant.23.clone.lat_back) | copy-start | bytes 7077892
  4.2 85.2 %copy-start.3 = (bf16[512,384]{1,0:T(8,128)(2,1)S(1)}, bf16[512,384]{1,0:T(8,128)(2,1)}, u32[]{:S(2)}) copy-start(bf16[512,384]{1,0:T(8,128)(2,1)} %constant.18.clone.lon_odd) | copy-start | bytes 1179652
  4.2 85.2 %copy-start.4 = (bf16[384,512]{1,0:T(8,128)(2,1)S(1)}, bf16[384,512]{1,0:T(8,128)(2,1)}, u32[]{:S(2)}) copy-start(bf16[384,512]{1,0:T(8,128)(2,1)} %constant.21.clone.back_odd) | copy-start | bytes 1179652
  4.2 85.2 %copy-start.7 = (bf16[256,256]{1,0:T(8,128)(2,1)S(1)}, bf16[256,256]{1,0:T(8,128)(2,1)}, u32[]{:S(2)}) copy-start(bf16[256,256]{1,0:T(8,128)(2,1)} %constant.16.clone.lon_zero) | copy-start | bytes 393220
  4.2 85.2 %copy-start.8 = (bf16[256,256]{1,0:T(8,128)(2,1)S(1)}, bf16[256,256]{1,0:T(8,128)(2,1)}, u32[]{:S(2)}) copy-start(bf16[256,256]{1,0:T(8,128)(2,1)} %constant.17.clone.lon_two) | copy-start | bytes 393220
  4.3 85.2 %copy-start.9 = (bf16[256,256]{1,0:T(8,128)(2,1)S(1)}, bf16[256,256]{1,0:T(8,128)(2,1)}, u32[]{:S(2)}) copy-start(bf16[256,256]{1,0:T(8,128)(2,1)} %constant.19.clone.back_zero) | copy-start | bytes 393220
  4.3 85.2 %copy-start.10 = (bf16[256,256]{1,0:T(8,128)(2,1)S(1)}, bf16[256,256]{1,0:T(8,128)(2,1)}, u32[]{:S(2)}) copy-start(bf16[256,256]{1,0:T(8,128)(2,1)} %constant.20.clone.back_two) | copy-start | bytes 393220
  4.3 85.2 %copy-start.12 = (f32[2,384]{1,0:T(2,128)S(1)}, f32[2,384]{1,0:T(2,128)}, u32[]{:S(2)}) copy-start(f32[2,384]{1,0:T(2,128)} %weight.2) | copy-start | bytes 9220
  87.1 12.7 %collective-permute-start = (bf16[720,128]{1,0:T(8,128)(2,1)S(1)}, bf16[720,128]{1,0:T(8,128)(2,1)S(1)}, u32[]{:S(2)}, u32[]{:S(2)}) collective-permute-start(bf16[720,128]{1,0:T(8,128)(2,1)S(1)} %bitcast.13), channel_id=1, source_target_pairs={{0,64},{64,0},{1,65},{65,1},{2,66},{66,2},{3,67},{67,3},{4,68},{68... | collective-permute-start | bytes 552968 | tf_op jit(solution)/shard_map/ppermute | solution.py:727
  87.5 12.3 %collective-permute-start.1 = (bf16[1,76,128]{2,1,0:T(8,128)(2,1)S(1)}, bf16[1,76,128]{2,1,0:T(8,128)(2,1)S(1)}, u32[]{:S(2)}, u32[]{:S(2)}) collective-permute-start(bf16[1,76,128]{2,1,0:T(8,128)(2,1)S(1)} %get-tuple-element.32), channel_id=1, source_target_pairs={{0,8},{8,0},{16,24},{24,16},{32,40},{40,32},{48,56},{56,48},{1,9},... | collective-permute-start | bytes 58376 | tf_op jit(solution)/shard_map/ppermute | solution.py:728
  88.5 11.2 %collective-permute-start.2 = (bf16[1,76,128]{2,1,0:T(8,128)(2,1)S(1)}, bf16[1,76,128]{2,1,0:T(8,128)(2,1)S(1)}, u32[]{:S(2)}, u32[]{:S(2)}) collective-permute-start(bf16[1,76,128]{2,1,0:T(8,128)(2,1)S(1)} %get-tuple-element.33), channel_id=1, source_target_pairs={{8,16},{16,8},{24,32},{32,24},{40,48},{48,40},{9,17},{17,9},{25,33... | collective-permute-start | bytes 58376 | tf_op jit(solution)/shard_map/ppermute | solution.py:729
  99.8 81.7 %copy-start = (bf16[76,90,128]{2,0,1:T(8,128)(2,1)S(1)}, bf16[76,90,128]{2,0,1:T(8,128)(2,1)}, u32[]{:S(2)}) copy-start(bf16[76,90,128]{2,0,1:T(8,128)(2,1)} %param.19) | copy-start | bytes 5253124
  99.8 81.7 %copy-start.11 = (bf16[128,76]{0,1:T(8,128)(2,1)S(1)}, bf16[128,76]{0,1:T(8,128)(2,1)}, u32[]{:S(2)}) copy-start(bf16[128,76]{0,1:T(8,128)(2,1)} %param.25) | copy-start | bytes 58372
  99.8 81.7 %copy-start.13 = (bf16[4,128]{1,0:T(4,128)(2,1)S(1)}, bf16[4,128]{1,0:T(4,128)(2,1)}, u32[]{:S(2)}) copy-start(bf16[4,128]{1,0:T(4,128)(2,1)} %weight.3) | copy-start | bytes 3076
  184.4 10.7 %collective-permute-start.3 = (bf16[448,128]{1,0:T(8,128)(2,1)S(1)}, bf16[448,128]{1,0:T(8,128)(2,1)S(1)}, u32[]{:S(2)}, u32[]{:S(2)}) collective-permute-start(bf16[448,128]{1,0:T(8,128)(2,1)S(1)} %get-tuple-element.43.own), channel_id=1, source_target_pairs={{0,64},{64,0},{1,65},{65,1},{2,66},{66,2},{3,67},{67,3},{4,68},{68... | collective-permute-start | bytes 344072 | tf_op jit(solution)/shard_map/ppermute | solution.py:746
  184.9 10.1 %collective-permute-start.4 = (bf16[448,128]{1,0:T(8,128)(2,1)S(1)}, bf16[448,128]{1,0:T(8,128)(2,1)S(1)}, u32[]{:S(2)}, u32[]{:S(2)}) collective-permute-start(bf16[448,128]{1,0:T(8,128)(2,1)S(1)} %get-tuple-element.44), channel_id=1, source_target_pairs={{0,1},{1,0},{2,3},{3,2},{4,5},{5,4},{6,7},{7,6},{8,9},{9,8},{10,11... | collective-permute-start | bytes 344072 | tf_op jit(solution)/shard_map/ppermute | solution.py:747
  186.0 9.1 %collective-permute-start.6 = (bf16[448,128]{1,0:T(8,128)(2,1)S(1)}, bf16[448,128]{1,0:T(8,128)(2,1)S(1)}, u32[]{:S(2)}, u32[]{:S(2)}) collective-permute-start(bf16[448,128]{1,0:T(8,128)(2,1)S(1)} %get-tuple-element.45), channel_id=1, source_target_pairs={{0,7},{1,2},{2,1},{3,4},{4,3},{5,6},{6,5},{7,0},{8,15},{9,10},{10,... | collective-permute-start | bytes 344072 | tf_op jit(solution)/shard_map/ppermute | solution.py:749
  187.9 7.2 %copy-start.5 = (s32[90,128]{1,0:T(8,128)S(1)}, s32[90,128]{1,0:T(8,128)}, u32[]{:S(2)}) copy-start(s32[90,128]{1,0:T(8,128)} %mask.3) | copy-start | bytes 138244
  187.9 5.3 %collective-permute-start.5 = (bf16[368,128]{1,0:T(8,128)(2,1)S(1)}, bf16[368,128]{1,0:T(8,128)(2,1)S(1)}, u32[]{:S(2)}, u32[]{:S(2)}) collective-permute-start(bf16[368,128]{1,0:T(8,128)(2,1)S(1)} %get-tuple-element.38), channel_id=1, source_target_pairs={{0,65},{1,64},{2,67},{3,66},{4,69},{5,68},{6,71},{7,70},{64,1},{65... | collective-permute-start | bytes 282632 | tf_op jit(solution)/shard_map/ppermute | solution.py:748
  189.7 5.4 %collective-permute-start.7 = (bf16[368,128]{1,0:T(8,128)(2,1)S(1)}, bf16[368,128]{1,0:T(8,128)(2,1)S(1)}, u32[]{:S(2)}, u32[]{:S(2)}) collective-permute-start(bf16[368,128]{1,0:T(8,128)(2,1)S(1)} %get-tuple-element.38), channel_id=1, source_target_pairs={{0,71},{1,66},{2,65},{3,68},{4,67},{5,70},{6,69},{7,64},{64,7},{65... | collective-permute-start | bytes 282632 | tf_op jit(solution)/shard_map/ppermute | solution.py:750

commit v5 on v4

--- a/solution.py
+++ b/solution.py
@@ -475,7 +475,7 @@
         0, ROWS, lambda row, kept: gather(row + 1, ocean[row], kept), edges, unroll=18
     )
 
-    sums = found[...].astype(BF16)
+    sums = found[0:368, :].astype(BF16)
     flux[...] = sums
     near_edge = jnp.where(even("lon"), edges[0], edges[1])
     far_edge = jnp.where(even("lon"), edges[1], edges[0])
@@ -546,7 +546,7 @@
         scratch_shapes=unpack_scratch()
         + [
             pltpu.VMEM((2, CH, COLS), F32),
-            pltpu.VMEM((368, COLS), F32),
+            pltpu.VMEM((376, COLS), F32),
             pltpu.SemaphoreType.DMA((6,)),
         ],
         compiler_params=pltpu.CompilerParams(vmem_limit_bytes=12 * MIB),
@@ -602,9 +602,9 @@
     west, east = sides(whole(near_one, near_other), whole(far_one, far_other))
     west = pltpu.roll(west, 1, 1)
     east = pltpu.roll(east, COLS - 1, 1)
-    fluxes[0] = jnp.where(column == 0, west, pltpu.roll(middle, 1, 1))
-    fluxes[1] = middle
-    fluxes[2] = jnp.where(column == COLS - 1, east, pltpu.roll(middle, COLS - 1, 1))
+    fluxes[0, 0:368, :] = jnp.where(column == 0, west, pltpu.roll(middle, 1, 1))
+    fluxes[1, 0:368, :] = middle
+    fluxes[2, 0:368, :] = jnp.where(column == COLS - 1, east, pltpu.roll(middle, COLS - 1, 1))
 
     head[:, 0:128] = own[368:448, :]
     head[:, 128:256] = other[368:448, :]
@@ -685,7 +685,7 @@
         scratch_shapes=[
             pltpu.VMEM((92 * 240 + 48, COLS), BF16),
             pltpu.VMEM((80, 256), BF16),
-            pltpu.VMEM((3, 368, COLS), F32),
+            pltpu.VMEM((3, 376, COLS), F32),
             pltpu.VMEM((2, 256, 1280), BF16),
             pltpu.VMEM((ROWS, 76, COLS), BF16),
             pltpu.SemaphoreType.DMA((9,)),

time: 203 us -> 203 us (level)
  no operation moved by 1% of the time
where the time goes in v5:
time: 203 us
  blocking collectives  164 us (81%)
  Pallas kernels  26.9 us (13%)
  starting transfers between devices  7.57 us (4%)
  waiting for transfers between devices  2.96 us (1%)
    all_to_all x1, blocking collectives, local(): lax.all_to_all(sent, ('lat', 'lon'), split_axis=0, concat_axis=0, tiled=T...  82.8 us
    all_to_all x1, blocking collectives, local(): lax.all_to_all(sent_back, ('lat', 'lon'), split_axis=0, concat_axis=0, ti...  81.7 us
    pallas_call x1, Pallas kernels, spectral(): pl.pallas_call(spectral_kernel, in_specs=[vmem()] * 10, out_specs=[vmem()...  10.3 us
    pallas_call x1, Pallas kernels, ocean_step(): pl.pallas_call(ocean_kernel, in_specs=[vmem()] * 10, out_specs=in_hbm(),...  7.85 us
  transfers between devices with their start and end apart: 8, of which 2 were waited for; matrix products, arithmetic and copies ran while one was open for 0% of the time, Pallas kernels for 6%

profile of v5, /device:TPU:1, one launch (start us, length us, event | category | flops | bytes accessed | tf_op | source)
XLA Modules:
  0.0 203.1 jit_solution(6241480961517825938)
XLA Ops:
  0.6 3.5 %pack.1 = (bf16[64,360,128]{2,1,0:T(8,128)(2,1)S(1)}, bf16[1,76,128]{2,1,0:T(8,128)(2,1)S(1)}, bf16[1,76,128]{2,1,0:T(8,128)(2,1)S(1)}) custom-call(bf16[90,128,128]{2,1,0:T(8,128)(2,1)} %bitcast.16, bf16[90,128,128]{2,1,0:T(8,128)(2,1)} %bitcast.17, bf16[90,76,128]{2,1,0:T(8,128)(2,1)} %bitcast.9, s32[90,128]{1,0:T(8,128)} %mask.3, f32[1,128]{1,0:T(1,128)} %bitcast.19), custom_call_target="tpu_custom_call" | custom-call | tf_op jit(solution)/shard_map/pack/pallas_call | solution.py:176
  4.2 0.0 copy-start.6
  4.2 0.0 copy-start.1
  4.2 0.0 copy-start.2
  4.2 0.0 copy-start.3
  4.2 0.0 copy-start.4
  4.2 0.0 copy-start.7
  4.2 0.0 copy-start.8
  4.3 0.0 copy-start.9
  4.3 0.0 copy-start.10
  4.3 0.0 copy-start.12
  4.3 82.8 %all_to_all.10.got = bf16[64,360,128]{2,1,0:T(8,128)(2,1)S(1)} all-to-all(bf16[64,360,128]{2,1,0:T(8,128)(2,1)S(1)} %get-tuple-element.26), channel_id=1, replica_groups=mesh['group'=2,'lat'=8,'lon'=8] {'lat','lon'}, dimensions={0} | all-to-all | bytes 11796480 | tf_op jit(solution)/shard_map/all_to_all | solution.py:723
  87.1 0.0 copy-done.6
  87.1 0.4 collective-permute-start
  87.5 1.1 collective-permute-start.1
  88.5 0.8 collective-permute-start.2
  89.4 0.0 copy-done.1
  89.4 0.0 copy-done.2
  89.4 0.0 copy-done.3
  89.4 0.0 copy-done.4
  89.4 0.0 copy-done.7
  89.4 0.0 copy-done.8
  89.4 0.0 copy-done.9
  89.5 0.0 copy-done.10
  89.5 0.0 copy-done.12
  89.5 10.3 %spectral.1 = (bf16[64,368,128]{2,1,0:T(8,128)(2,1)S(1)}, f32[2,384]{1,0:T(2,128)}) custom-call(bf16[64,360,128]{2,1,0:T(8,128)(2,1)S(1)} %all_to_all.10.got, bf16[256,256]{1,0:T(8,128)(2,1)S(1)} %copy-done.7, bf16[256,256]{1,0:T(8,128)(2,1)S(1)} %copy-done.8, bf16[512,384]{1,0:T(8,128)(2,1)S(1)} %copy-done.3, bf16[256,256]{1,0:T(8,128)(2,1)S(1)} %copy-done.9, ...), custom_call_target="tpu_custom_call" | custom-call | tf_op jit(solution)/shard_map/spectral/pallas_call | solution.py:358
  99.8 0.0 collective-permute-done.1.got_one
  99.8 0.0 collective-permute-done.2.got_two
  99.8 0.0 collective-permute-done.weights_other
  99.8 0.0 copy-start
  99.8 0.0 copy-start.11
  99.8 0.0 copy-start.13
  99.8 81.7 %all_to_all.11.sent_back = bf16[64,368,128]{2,1,0:T(8,128)(2,1)S(1)} all-to-all(bf16[64,368,128]{2,1,0:T(8,128)(2,1)S(1)} %get-tuple-element.34), channel_id=1, replica_groups=mesh['group'=2,'lat'=8,'lon'=8] {'lat','lon'}, dimensions={0} | all-to-all | bytes 12058624 | tf_op jit(solution)/shard_map/all_to_all | solution.py:736
  181.5 0.0 copy-done
  181.5 2.8 %unpack_flux.1 = (bf16[90,128,128]{2,1,0:T(8,128)(2,1)}, bf16[368,128]{1,0:T(8,128)(2,1)S(1)}, bf16[448,128]{1,0:T(8,128)(2,1)S(1)}, bf16[448,128]{1,0:T(8,128)(2,1)S(1)}, bf16[448,128]{1,0:T(8,128)(2,1)S(1)}) custom-call(bf16[64,368,128]{2,1,0:T(8,128)(2,1)S(1)} %all_to_all.11.sent_back, bf16[4,128]{1,0:T(4,128)(2,1)S(1)} %copy-done.13, ...), custom_call_target="tpu_custom_call" | custom-call | tf_op jit(solution)/shard_map/unpack_flux/pallas_call | solution.py:535
  184.4 0.6 collective-permute-start.3
  184.9 1.1 collective-permute-start.4
  186.0 1.9 collective-permute-start.6
  187.9 1.8 collective-permute-start.5
  189.7 0.0 collective-permute-start.7
  189.7 2.4 %unpack_taps.1 = (bf16[90,128,128]{2,1,0:T(8,128)(2,1)}, bf16[22128,128]{1,0:T(8,128)(2,1)S(1)}, bf16[256,768]{1,0:T(8,128)(2,1)S(1)}) custom-call(bf16[64,368,128]{2,1,0:T(8,128)(2,1)S(1)} %all_to_all.11.sent_back, bf16[720,128]{1,0:T(8,128)(2,1)S(1)} %bitcast.14, bf16[720,128]{1,0:T(8,128)(2,1)S(1)} %collective-permute-done.weights_other, ...), custom_call_target="tpu_custom_call" | custom-call | bytes 12000000 | tf_op jit(solution)/shard_map/unpack_taps/pallas_call | solution.py:558
  192.1 1.1 collective-permute-done.5.near_other
  193.2 1.8 collective-permute-done.7.far_other
  195.0 0.0 collective-permute-done.3.other
  195.1 0.0 collective-permute-done.4.near_one
  195.1 0.0 collective-permute-done.6.far_one
  195.1 0.0 copy-done.5
  195.1 7.8 %ocean.1 = bf16[90,76,128]{2,1,0:T(8,128)(2,1)} custom-call(bf16[448,128]{1,0:T(8,128)(2,1)S(1)} %get-tuple-element.43.own, bf16[448,128]{1,0:T(8,128)(2,1)S(1)} %collective-permute-done.3.other, bf16[448,128]{1,0:T(8,128)(2,1)S(1)} %collective-permute-done.4.near_one, bf16[368,128]{1,0:T(8,128)(2,1)S(1)} %collective-permute-done.5.near_other, ...), custom_call_target="tpu_custom_call" | custom-call | tf_op jit(solution)/shard_map/ocean/pallas_call | solution.py:680
  (3 shorter events, 0.0 us)
Async XLA Ops:
  4.2 82.9 %copy-start.6 = (bf16[3,3,80,128]{3,2,1,0:T(8,128)(2,1)S(1)}, bf16[3,3,80,128]{3,2,1,0:T(8,128)(2,1)}, u32[]{:S(2)}) copy-start(bf16[3,3,80,128]{3,2,1,0:T(8,128)(2,1)} %param.24) | copy-start | bytes 552964
  4.2 85.2 %copy-start.1 = (bf16[4,384,768]{2,1,0:T(8,128)(2,1)S(1)}, bf16[4,384,768]{2,1,0:T(8,128)(2,1)}, u32[]{:S(2)}) copy-start(bf16[4,384,768]{2,1,0:T(8,128)(2,1)} %constant.22.clone.lat) | copy-start | bytes 7077892
  4.2 85.2 %copy-start.2 = (bf16[4,768,384]{2,1,0:T(8,128)(2,1)S(1)}, bf16[4,768,384]{2,1,0:T(8,128)(2,1)}, u32[]{:S(2)}) copy-start(bf16[4,768,384]{2,1,0:T(8,128)(2,1)} %constant.23.clone.lat_back) | copy-start | bytes 7077892
  4.2 85.2 %copy-start.3 = (bf16[512,384]{1,0:T(8,128)(2,1)S(1)}, bf16[512,384]{1,0:T(8,128)(2,1)}, u32[]{:S(2)}) copy-start(bf16[512,384]{1,0:T(8,128)(2,1)} %constant.18.clone.lon_odd) | copy-start | bytes 1179652
  4.2 85.2 %copy-start.4 = (bf16[384,512]{1,0:T(8,128)(2,1)S(1)}, bf16[384,512]{1,0:T(8,128)(2,1)}, u32[]{:S(2)}) copy-start(bf16[384,512]{1,0:T(8,128)(2,1)} %constant.21.clone.back_odd) | copy-start | bytes 1179652
  4.2 85.2 %copy-start.7 = (bf16[256,256]{1,0:T(8,128)(2,1)S(1)}, bf16[256,256]{1,0:T(8,128)(2,1)}, u32[]{:S(2)}) copy-start(bf16[256,256]{1,0:T(8,128)(2,1)} %constant.16.clone.lon_zero) | copy-start | bytes 393220
  4.2 85.2 %copy-start.8 = (bf16[256,256]{1,0:T(8,128)(2,1)S(1)}, bf16[256,256]{1,0:T(8,128)(2,1)}, u32[]{:S(2)}) copy-start(bf16[256,256]{1,0:T(8,128)(2,1)} %constant.17.clone.lon_two) | copy-start | bytes 393220
  4.3 85.2 %copy-start.9 = (bf16[256,256]{1,0:T(8,128)(2,1)S(1)}, bf16[256,256]{1,0:T(8,128)(2,1)}, u32[]{:S(2)}) copy-start(bf16[256,256]{1,0:T(8,128)(2,1)} %constant.19.clone.back_zero) | copy-start | bytes 393220
  4.3 85.2 %copy-start.10 = (bf16[256,256]{1,0:T(8,128)(2,1)S(1)}, bf16[256,256]{1,0:T(8,128)(2,1)}, u32[]{:S(2)}) copy-start(bf16[256,256]{1,0:T(8,128)(2,1)} %constant.20.clone.back_two) | copy-start | bytes 393220
  4.3 85.2 %copy-start.12 = (f32[2,384]{1,0:T(2,128)S(1)}, f32[2,384]{1,0:T(2,128)}, u32[]{:S(2)}) copy-start(f32[2,384]{1,0:T(2,128)} %weight.2) | copy-start | bytes 9220
  87.1 12.7 %collective-permute-start = (bf16[720,128]{1,0:T(8,128)(2,1)S(1)}, bf16[720,128]{1,0:T(8,128)(2,1)S(1)}, u32[]{:S(2)}, u32[]{:S(2)}) collective-permute-start(bf16[720,128]{1,0:T(8,128)(2,1)S(1)} %bitcast.13), channel_id=1, source_target_pairs={{0,64},{64,0},{1,65},{65,1},{2,66},{66,2},{3,67},{67,3},{4,68},{68... | collective-permute-start | bytes 552968 | tf_op jit(solution)/shard_map/ppermute | solution.py:727
  87.5 12.3 %collective-permute-start.1 = (bf16[1,76,128]{2,1,0:T(8,128)(2,1)S(1)}, bf16[1,76,128]{2,1,0:T(8,128)(2,1)S(1)}, u32[]{:S(2)}, u32[]{:S(2)}) collective-permute-start(bf16[1,76,128]{2,1,0:T(8,128)(2,1)S(1)} %get-tuple-element.32), channel_id=1, source_target_pairs={{0,8},{8,0},{16,24},{24,16},{32,40},{40,32},{48,56},{56,48},{1,9},... | collective-permute-start | bytes 58376 | tf_op jit(solution)/shard_map/ppermute | solution.py:728
  88.5 11.2 %collective-permute-start.2 = (bf16[1,76,128]{2,1,0:T(8,128)(2,1)S(1)}, bf16[1,76,128]{2,1,0:T(8,128)(2,1)S(1)}, u32[]{:S(2)}, u32[]{:S(2)}) collective-permute-start(bf16[1,76,128]{2,1,0:T(8,128)(2,1)S(1)} %get-tuple-element.33), channel_id=1, source_target_pairs={{8,16},{16,8},{24,32},{32,24},{40,48},{48,40},{9,17},{17,9},{25,33... | collective-permute-start | bytes 58376 | tf_op jit(solution)/shard_map/ppermute | solution.py:729
  99.8 81.7 %copy-start = (bf16[76,90,128]{2,0,1:T(8,128)(2,1)S(1)}, bf16[76,90,128]{2,0,1:T(8,128)(2,1)}, u32[]{:S(2)}) copy-start(bf16[76,90,128]{2,0,1:T(8,128)(2,1)} %param.19) | copy-start | bytes 5253124
  99.8 81.7 %copy-start.11 = (bf16[128,76]{0,1:T(8,128)(2,1)S(1)}, bf16[128,76]{0,1:T(8,128)(2,1)}, u32[]{:S(2)}) copy-start(bf16[128,76]{0,1:T(8,128)(2,1)} %param.25) | copy-start | bytes 58372
  99.8 81.7 %copy-start.13 = (bf16[4,128]{1,0:T(4,128)(2,1)S(1)}, bf16[4,128]{1,0:T(4,128)(2,1)}, u32[]{:S(2)}) copy-start(bf16[4,128]{1,0:T(4,128)(2,1)} %weight.3) | copy-start | bytes 3076
  184.4 10.7 %collective-permute-start.3 = (bf16[448,128]{1,0:T(8,128)(2,1)S(1)}, bf16[448,128]{1,0:T(8,128)(2,1)S(1)}, u32[]{:S(2)}, u32[]{:S(2)}) collective-permute-start(bf16[448,128]{1,0:T(8,128)(2,1)S(1)} %get-tuple-element.43.own), channel_id=1, source_target_pairs={{0,64},{64,0},{1,65},{65,1},{2,66},{66,2},{3,67},{67,3},{4,68},{68... | collective-permute-start | bytes 344072 | tf_op jit(solution)/shard_map/ppermute | solution.py:746
  184.9 10.1 %collective-permute-start.4 = (bf16[448,128]{1,0:T(8,128)(2,1)S(1)}, bf16[448,128]{1,0:T(8,128)(2,1)S(1)}, u32[]{:S(2)}, u32[]{:S(2)}) collective-permute-start(bf16[448,128]{1,0:T(8,128)(2,1)S(1)} %get-tuple-element.44), channel_id=1, source_target_pairs={{0,1},{1,0},{2,3},{3,2},{4,5},{5,4},{6,7},{7,6},{8,9},{9,8},{10,11... | collective-permute-start | bytes 344072 | tf_op jit(solution)/shard_map/ppermute | solution.py:747
  186.0 9.1 %collective-permute-start.6 = (bf16[448,128]{1,0:T(8,128)(2,1)S(1)}, bf16[448,128]{1,0:T(8,128)(2,1)S(1)}, u32[]{:S(2)}, u32[]{:S(2)}) collective-permute-start(bf16[448,128]{1,0:T(8,128)(2,1)S(1)} %get-tuple-element.45), channel_id=1, source_target_pairs={{0,7},{1,2},{2,1},{3,4},{4,3},{5,6},{6,5},{7,0},{8,15},{9,10},{10,... | collective-permute-start | bytes 344072 | tf_op jit(solution)/shard_map/ppermute | solution.py:749
  187.9 7.2 %copy-start.5 = (s32[90,128]{1,0:T(8,128)S(1)}, s32[90,128]{1,0:T(8,128)}, u32[]{:S(2)}) copy-start(s32[90,128]{1,0:T(8,128)} %mask.3) | copy-start | bytes 138244
  187.9 5.3 %collective-permute-start.5 = (bf16[368,128]{1,0:T(8,128)(2,1)S(1)}, bf16[368,128]{1,0:T(8,128)(2,1)S(1)}, u32[]{:S(2)}, u32[]{:S(2)}) collective-permute-start(bf16[368,128]{1,0:T(8,128)(2,1)S(1)} %get-tuple-element.38), channel_id=1, source_target_pairs={{0,65},{1,64},{2,67},{3,66},{4,69},{5,68},{6,71},{7,70},{64,1},{65... | collective-permute-start | bytes 282632 | tf_op jit(solution)/shard_map/ppermute | solution.py:748
  189.7 5.4 %collective-permute-start.7 = (bf16[368,128]{1,0:T(8,128)(2,1)S(1)}, bf16[368,128]{1,0:T(8,128)(2,1)S(1)}, u32[]{:S(2)}, u32[]{:S(2)}) collective-permute-start(bf16[368,128]{1,0:T(8,128)(2,1)S(1)} %get-tuple-element.38), channel_id=1, source_target_pairs={{0,71},{1,66},{2,65},{3,68},{4,67},{5,70},{6,69},{7,64},{64,7},{65... | collective-permute-start | bytes 282632 | tf_op jit(solution)/shard_map/ppermute | solution.py:750
